TPU v7x, 32 devices: a whole 2x2x4 slice. The times are simulated.
32 devices in a mesh: cell: 8 (over z, core), sub: 4 (over y, x).
Axes of the slice: x: 2, y: 2, z: 4, core: 2. Of those that a mesh axis runs over, the one named last changes fastest.
Arguments:
- queries: bfloat16 [2048, 1024], P('cell', 'sub'), may hold values from -384 to 384
- probe_groups: int32 [2048, 2], P('cell'), may hold values from 0 to 7, all different within a row; in each aligned block of 256 rows (0 to 255, 256 to 511, ...) at most 64 rows name the same one
- probe_cells: int32 [2048, 2, 16], P('cell'), may hold values from 0 to 31, as said below
- coarse: bfloat16 [256, 1024], P('cell', 'sub'), may hold values from -1.1953125 to 1.1953125
- codebooks: bfloat16 [64, 16, 256], P('sub'), may hold values from -1.5 to 1.5
- codes: int32 [256, 64, 384], P('cell', 'sub'), may hold values from 0 to 255
- lengths: int32 [256], P('cell'), may hold values from 1 to 384, 49152 in all
- payload: bfloat16 [256, 384, 256], P('cell', 'sub'), may hold values from -6 to 6
Outputs:
- pooled: bfloat16 [2048, 256], P('cell')
Inputs may be any that keep to these rules, and one draw needn't show every extreme that they name: `probe_cells`: the 16 cells of one query in one group are distinct. `probe_groups`: the queries of one index of cell name one group at most 64 times, and one group exactly 64 times in some index. `lengths`: some cell has all 384 rows live.
All inputs are finite; a program needn't handle non-finite values. No bound on the sum of `lengths` on one device may be relied on, other than what follows from the above.
Results may differ from a plain program's by a relative error of at most 0.003.
The roundings to bfloat16 on the way count: a program that leaves them out, or rounds other values in their place, can miss the bound.
Values may be sent and summed in bfloat16 or wider, within the bound.
A program may use at most 64 MiB of HBM per device.

v0:
```python
import math

import jax
import jax.numpy as jnp
from jax import lax
from jax.sharding import PartitionSpec as P

CAP = 64


score_scale = 0.3
floor_score = -1e30


def slot_table(probe_groups, groups, capacity):
    marks = (probe_groups[:, :, None] == jnp.arange(groups, dtype=jnp.int32)[None, None, :]).astype(
        jnp.int32
    )
    routed = jnp.sum(marks, axis=1)
    earlier = jnp.cumsum(routed, axis=0) - routed
    position = jnp.sum(marks * earlier[:, None, :], axis=2)
    return probe_groups * capacity + position


def pack_slots(rows, probe_cells, slots, total):
    flat = slots.reshape(-1)
    doubled = jnp.repeat(rows, 2, axis=0)
    buffer = jnp.zeros((total, rows.shape[1]), rows.dtype).at[flat].set(doubled)
    named = probe_cells.reshape(flat.shape[0], -1).astype(jnp.bfloat16)
    cell_marks = jnp.full((total, probe_cells.shape[2]), -1.0, jnp.bfloat16).at[flat].set(named)
    return (buffer, cell_marks)


def decode(coarse, codebooks, codes):
    cell_count = codes.shape[0]
    sub_count = codes.shape[1]
    row_count = codes.shape[2]
    width = codebooks.shape[1]
    centroid_ids = jnp.arange(codebooks.shape[2], dtype=jnp.int32)

    def one_subspace(pair):
        book = pair[0]
        flat_codes = pair[1].reshape(-1)
        onehot = (flat_codes[None, :] == centroid_ids[:, None]).astype(jnp.bfloat16)
        return jnp.dot(book, onehot, preferred_element_type=jnp.float32)

    picked = lax.map(one_subspace, (codebooks, jnp.transpose(codes, (1, 0, 2))))
    recon = picked.reshape(sub_count * width, cell_count, row_count)
    return (recon + coarse.T.astype(jnp.float32)[:, :, None]).astype(jnp.bfloat16)


def combine(back_part, back_mass, back_peak, slots, total):
    peaks = back_peak.reshape(-1)[slots]
    masses = back_mass.reshape(-1)[slots]
    parts = back_part.reshape(total, -1)[slots]
    top = jnp.max(peaks, axis=1, keepdims=True)
    scale = jnp.exp(peaks - top)
    upper = jnp.sum(scale[:, :, None] * parts, axis=1)
    lower = jnp.sum(scale * masses, axis=1)
    return (upper / lower[:, None]).astype(jnp.bfloat16)


def local(queries, probe_groups, probe_cells, coarse, codebooks, codes, lengths, payload):
    groups = lax.axis_size("cell")
    capacity = CAP
    total = groups * capacity
    slots = slot_table(probe_groups, groups, capacity)
    buffer, cell_marks = pack_slots(queries, probe_cells, slots, total)
    arrived, arrived_cells = (
        lax.all_to_all(
            buffer.reshape(groups, capacity, -1), "cell", split_axis=0, concat_axis=0, tiled=True
        ),
        lax.all_to_all(
            cell_marks.reshape(groups, capacity, -1),
            "cell",
            split_axis=0,
            concat_axis=0,
            tiled=True,
        ),
    )
    full_rows = lax.all_gather(arrived.reshape(total, -1), "sub", axis=1, tiled=True)
    cell_ids = arrived_cells.reshape(total, -1).astype(jnp.int32)
    cell_dev = codes.shape[0]
    probed = jnp.any(
        cell_ids[:, :, None] == jnp.arange(cell_dev, dtype=jnp.int32)[None, None, :], axis=1
    )
    local_vectors = decode(coarse, codebooks, codes)
    decoded = lax.all_to_all(local_vectors, "sub", split_axis=2, concat_axis=0, tiled=True)
    row_local = decoded.shape[2]
    decoded = decoded.reshape(decoded.shape[0], -1)
    sq_norm = jnp.sum(jnp.square(decoded.astype(jnp.float32)), axis=0)
    first_row = lax.axis_index("sub") * row_local
    live = (first_row + jnp.arange(row_local, dtype=jnp.int32))[None, :] < lengths[:, None]
    block = math.gcd(total, 512)
    count = total // block
    query_blocks = full_rows.reshape(count, block, -1)
    probe_blocks = probed.reshape(count, block, cell_dev)
    table = payload.reshape(-1, payload.shape[2])

    def block_scores(pair):
        raw = jnp.dot(pair[0], decoded, preferred_element_type=jnp.float32)
        values = (raw - 0.5 * sq_norm[None, :]) * score_scale
        keep = (pair[1][:, :, None] & live[None, :, :]).reshape(pair[0].shape[0], -1)
        return (values, keep, jnp.max(jnp.where(keep, values, floor_score), axis=1))

    value_blocks, keep_blocks, local_peak = lax.map(block_scores, (query_blocks, probe_blocks))
    peak = lax.pmax(local_peak.reshape(total), "sub")

    def block_sums(triple):
        weights = jnp.where(triple[1], jnp.exp(triple[0] - triple[2][:, None]), 0.0).astype(
            jnp.bfloat16
        )
        mass = jnp.sum(weights.astype(jnp.float32), axis=1)
        part = jnp.dot(weights, table, preferred_element_type=jnp.float32)
        return (mass, part)

    mass, part = lax.map(block_sums, (value_blocks, keep_blocks, peak.reshape(count, block)))
    mass = mass.reshape(total)
    part = part.reshape(total, -1)
    part_sum, mass_sum = lax.psum((part, mass), "sub")
    back_part, back_mass, back_peak = (
        lax.all_to_all(
            part_sum.reshape(groups, capacity, -1), "cell", split_axis=0, concat_axis=0, tiled=True
        ),
        lax.all_to_all(
            mass_sum.reshape(groups, capacity), "cell", split_axis=0, concat_axis=0, tiled=True
        ),
        lax.all_to_all(
            peak.reshape(groups, capacity), "cell", split_axis=0, concat_axis=0, tiled=True
        ),
    )
    return combine(back_part, back_mass, back_peak, slots, total)


def solution(mesh):
    placed = (
        P("cell", "sub"),
        P("cell", None),
        P("cell", None, None),
        P("cell", "sub"),
        P("sub", None, None),
        P("cell", "sub", None),
        P("cell"),
        P("cell", "sub", None),
    )
    return jax.shard_map(
        local, mesh=mesh, in_specs=placed, out_specs=P("cell", None), check_vma=False
    )
```

profile of v0, /device:TPU:0, one launch (start us, length us, event | category | flops | bytes accessed | tf_op | source)
XLA Modules:
  0.0 333.8 jit_solution(4371366986496107622)
XLA Ops:
  6.5 0.8 convert_reduce_fusion.1
  7.3 0.6 reduce-window.6
  7.9 0.2 slice_reduce_fusion
  8.2 0.7 select_reduce_fusion.1
  9.0 0.7 compare_select_fusion.1
  9.9 0.8 convert_element_type.52
  10.8 1.8 scatter_custom_fusion
  12.7 0.7 reshape.308
  13.4 6.3 %all-to-all-start = ((bf16[8,2,512]{2,1,0:T(2,128)(2,1)}), bf16[8,2,512]{2,1,0:T(2,128)(2,1)S(1)}, u32[]{:S(2)}, u32[]{:S(2)}) async-start(bf16[8,2,512]{2,1,0:T(2,128)(2,1)} %reshape.308), calls=%async_computation | async-start | bytes 32768 | tf_op jit(solution)/shard_map/all_to_all | solution.py:73
  19.8 1.4 copy.120
  21.2 57.1 %while.3 = (s32[]{:T(128)}, f32[16,16,12288]{2,1,0:T(8,128)}, bf16[16,16,256]{2,1,0:T(8,128)(2,1)}, s32[16,32,384]{2,1,0:T(8,128)S(1)}, s32[]{:T(128)}) while((s32[]{:T(128)}, f32[16,16,12288]{2,1,0:T(8,128)}, bf16[16,16,256]{2,1,0:T(8,128)(2,1)}, s32[16,32,384]{2,1,0:T(8,128)S(1)}, s32[]{:T(128)}) %tuple.36), condition=%wide.region_8.9_spmd.clone, body=%wide.region_7.8_spmd.clone.sunk | while | flops 103809024 | bytes 1041481 | solution.py:47
  21.2 3.5 %fusion.24 = f32[16,16,12288]{2,1,0:T(8,128)} fusion(f32[16,16,12288]{2,1,0:T(8,128)} %get-tuple-element.138, s32[]{:T(128)S(6)} %copy.124, s32[12288]{0:T(1024)S(1)} %eq.81, bf16[16,16,256]{2,1,0:T(8,128)(2,1)} %get-tuple-element.144), kind=kOutput, calls=%fused_computation.7.clone.1 | convolution fusion | flops 103809024 | bytes 844800 | tf_op jit(solution)/shard_map/while/body/eval_jaxpr/dot_general | solution.py:45
  24.7 3.6 %fusion.24 = f32[16,16,12288]{2,1,0:T(8,128)} fusion(f32[16,16,12288]{2,1,0:T(8,128)} %get-tuple-element.138, s32[]{:T(128)S(6)} %copy.124, s32[12288]{0:T(1024)S(1)} %eq.81, bf16[16,16,256]{2,1,0:T(8,128)(2,1)} %get-tuple-element.144), kind=kOutput, calls=%fused_computation.7.clone.1 | convolution fusion | flops 103809024 | bytes 844800 | tf_op jit(solution)/shard_map/while/body/eval_jaxpr/dot_general | solution.py:45
  28.3 3.5 %fusion.24 = f32[16,16,12288]{2,1,0:T(8,128)} fusion(f32[16,16,12288]{2,1,0:T(8,128)} %get-tuple-element.138, s32[]{:T(128)S(6)} %copy.124, s32[12288]{0:T(1024)S(1)} %eq.81, bf16[16,16,256]{2,1,0:T(8,128)(2,1)} %get-tuple-element.144), kind=kOutput, calls=%fused_computation.7.clone.1 | convolution fusion | flops 103809024 | bytes 844800 | tf_op jit(solution)/shard_map/while/body/eval_jaxpr/dot_general | solution.py:45
  31.9 3.5 %fusion.24 = f32[16,16,12288]{2,1,0:T(8,128)} fusion(f32[16,16,12288]{2,1,0:T(8,128)} %get-tuple-element.138, s32[]{:T(128)S(6)} %copy.124, s32[12288]{0:T(1024)S(1)} %eq.81, bf16[16,16,256]{2,1,0:T(8,128)(2,1)} %get-tuple-element.144), kind=kOutput, calls=%fused_computation.7.clone.1 | convolution fusion | flops 103809024 | bytes 844800 | tf_op jit(solution)/shard_map/while/body/eval_jaxpr/dot_general | solution.py:45
  35.4 3.5 %fusion.24 = f32[16,16,12288]{2,1,0:T(8,128)} fusion(f32[16,16,12288]{2,1,0:T(8,128)} %get-tuple-element.138, s32[]{:T(128)S(6)} %copy.124, s32[12288]{0:T(1024)S(1)} %eq.81, bf16[16,16,256]{2,1,0:T(8,128)(2,1)} %get-tuple-element.144), kind=kOutput, calls=%fused_computation.7.clone.1 | convolution fusion | flops 103809024 | bytes 844800 | tf_op jit(solution)/shard_map/while/body/eval_jaxpr/dot_general | solution.py:45
  39.0 3.5 %fusion.24 = f32[16,16,12288]{2,1,0:T(8,128)} fusion(f32[16,16,12288]{2,1,0:T(8,128)} %get-tuple-element.138, s32[]{:T(128)S(6)} %copy.124, s32[12288]{0:T(1024)S(1)} %eq.81, bf16[16,16,256]{2,1,0:T(8,128)(2,1)} %get-tuple-element.144), kind=kOutput, calls=%fused_computation.7.clone.1 | convolution fusion | flops 103809024 | bytes 844800 | tf_op jit(solution)/shard_map/while/body/eval_jaxpr/dot_general | solution.py:45
  42.5 3.5 %fusion.24 = f32[16,16,12288]{2,1,0:T(8,128)} fusion(f32[16,16,12288]{2,1,0:T(8,128)} %get-tuple-element.138, s32[]{:T(128)S(6)} %copy.124, s32[12288]{0:T(1024)S(1)} %eq.81, bf16[16,16,256]{2,1,0:T(8,128)(2,1)} %get-tuple-element.144), kind=kOutput, calls=%fused_computation.7.clone.1 | convolution fusion | flops 103809024 | bytes 844800 | tf_op jit(solution)/shard_map/while/body/eval_jaxpr/dot_general | solution.py:45
  46.1 3.6 %fusion.24 = f32[16,16,12288]{2,1,0:T(8,128)} fusion(f32[16,16,12288]{2,1,0:T(8,128)} %get-tuple-element.138, s32[]{:T(128)S(6)} %copy.124, s32[12288]{0:T(1024)S(1)} %eq.81, bf16[16,16,256]{2,1,0:T(8,128)(2,1)} %get-tuple-element.144), kind=kOutput, calls=%fused_computation.7.clone.1 | convolution fusion | flops 103809024 | bytes 844800 | tf_op jit(solution)/shard_map/while/body/eval_jaxpr/dot_general | solution.py:45
  49.7 3.5 %fusion.24 = f32[16,16,12288]{2,1,0:T(8,128)} fusion(f32[16,16,12288]{2,1,0:T(8,128)} %get-tuple-element.138, s32[]{:T(128)S(6)} %copy.124, s32[12288]{0:T(1024)S(1)} %eq.81, bf16[16,16,256]{2,1,0:T(8,128)(2,1)} %get-tuple-element.144), kind=kOutput, calls=%fused_computation.7.clone.1 | convolution fusion | flops 103809024 | bytes 844800 | tf_op jit(solution)/shard_map/while/body/eval_jaxpr/dot_general | solution.py:45
  53.2 3.5 %fusion.24 = f32[16,16,12288]{2,1,0:T(8,128)} fusion(f32[16,16,12288]{2,1,0:T(8,128)} %get-tuple-element.138, s32[]{:T(128)S(6)} %copy.124, s32[12288]{0:T(1024)S(1)} %eq.81, bf16[16,16,256]{2,1,0:T(8,128)(2,1)} %get-tuple-element.144), kind=kOutput, calls=%fused_computation.7.clone.1 | convolution fusion | flops 103809024 | bytes 844800 | tf_op jit(solution)/shard_map/while/body/eval_jaxpr/dot_general | solution.py:45
  56.7 3.6 %fusion.24 = f32[16,16,12288]{2,1,0:T(8,128)} fusion(f32[16,16,12288]{2,1,0:T(8,128)} %get-tuple-element.138, s32[]{:T(128)S(6)} %copy.124, s32[12288]{0:T(1024)S(1)} %eq.81, bf16[16,16,256]{2,1,0:T(8,128)(2,1)} %get-tuple-element.144), kind=kOutput, calls=%fused_computation.7.clone.1 | convolution fusion | flops 103809024 | bytes 844800 | tf_op jit(solution)/shard_map/while/body/eval_jaxpr/dot_general | solution.py:45
  60.3 3.6 %fusion.24 = f32[16,16,12288]{2,1,0:T(8,128)} fusion(f32[16,16,12288]{2,1,0:T(8,128)} %get-tuple-element.138, s32[]{:T(128)S(6)} %copy.124, s32[12288]{0:T(1024)S(1)} %eq.81, bf16[16,16,256]{2,1,0:T(8,128)(2,1)} %get-tuple-element.144), kind=kOutput, calls=%fused_computation.7.clone.1 | convolution fusion | flops 103809024 | bytes 844800 | tf_op jit(solution)/shard_map/while/body/eval_jaxpr/dot_general | solution.py:45
  64.0 3.5 %fusion.24 = f32[16,16,12288]{2,1,0:T(8,128)} fusion(f32[16,16,12288]{2,1,0:T(8,128)} %get-tuple-element.138, s32[]{:T(128)S(6)} %copy.124, s32[12288]{0:T(1024)S(1)} %eq.81, bf16[16,16,256]{2,1,0:T(8,128)(2,1)} %get-tuple-element.144), kind=kOutput, calls=%fused_computation.7.clone.1 | convolution fusion | flops 103809024 | bytes 844800 | tf_op jit(solution)/shard_map/while/body/eval_jaxpr/dot_general | solution.py:45
  67.5 3.6 %fusion.24 = f32[16,16,12288]{2,1,0:T(8,128)} fusion(f32[16,16,12288]{2,1,0:T(8,128)} %get-tuple-element.138, s32[]{:T(128)S(6)} %copy.124, s32[12288]{0:T(1024)S(1)} %eq.81, bf16[16,16,256]{2,1,0:T(8,128)(2,1)} %get-tuple-element.144), kind=kOutput, calls=%fused_computation.7.clone.1 | convolution fusion | flops 103809024 | bytes 844800 | tf_op jit(solution)/shard_map/while/body/eval_jaxpr/dot_general | solution.py:45
  71.1 3.6 %fusion.24 = f32[16,16,12288]{2,1,0:T(8,128)} fusion(f32[16,16,12288]{2,1,0:T(8,128)} %get-tuple-element.138, s32[]{:T(128)S(6)} %copy.124, s32[12288]{0:T(1024)S(1)} %eq.81, bf16[16,16,256]{2,1,0:T(8,128)(2,1)} %get-tuple-element.144), kind=kOutput, calls=%fused_computation.7.clone.1 | convolution fusion | flops 103809024 | bytes 844800 | tf_op jit(solution)/shard_map/while/body/eval_jaxpr/dot_general | solution.py:45
  74.7 3.5 %fusion.24 = f32[16,16,12288]{2,1,0:T(8,128)} fusion(f32[16,16,12288]{2,1,0:T(8,128)} %get-tuple-element.138, s32[]{:T(128)S(6)} %copy.124, s32[12288]{0:T(1024)S(1)} %eq.81, bf16[16,16,256]{2,1,0:T(8,128)(2,1)} %get-tuple-element.144), kind=kOutput, calls=%fused_computation.7.clone.1 | convolution fusion | flops 103809024 | bytes 844800 | tf_op jit(solution)/shard_map/while/body/eval_jaxpr/dot_general | solution.py:45
  78.2 11.3 %copy.117 = f32[32,8,32,384]{3,2,1,0:T(8,128)} copy(f32[32,8,32,384]{3,1,2,0:T(8,128)} %bitcast.60) | data formatting | bytes 25165824
  89.9 3.0 scatter_custom_fusion.1
  92.9 5.1 %all-to-all-start.1 = ((bf16[8,64,256]{2,1,0:T(8,128)(2,1)}), bf16[8,64,256]{2,1,0:T(8,128)(2,1)S(1)}, u32[]{:S(2)}, u32[]{:S(2)}) async-start(bf16[8,64,256]{2,1,0:T(8,128)(2,1)} %bitcast.8), calls=%async_computation.1 | async-start | bytes 524288 | tf_op jit(solution)/shard_map/all_to_all | solution.py:70
  98.0 8.6 %fusion.7 = bf16[256,32,384]{2,1,0:T(8,128)(2,1)} fusion(f32[32,8,32,384]{3,2,1,0:T(8,128)} %copy.117, f32[256,32]{1,0:T(8,128)S(1)} %copy.107), kind=kLoop, calls=%fused_computation.15 | loop fusion | flops 6291456 | bytes 18907136 | tf_op jit(solution)/shard_map/convert_element_type | solution.py:49
  106.6 9.6 %copy.108 = bf16[256,32,384]{0,1,2:T(8,128)(2,1)} copy(bf16[256,32,384]{2,1,0:T(8,128)(2,1)} %fusion.7) | data formatting | bytes 12582912 | tf_op jit(solution)/shard_map/convert_element_type | solution.py:49
  116.2 0.7 copy-done.2
  116.9 5.2 %all-to-all-start.2 = ((bf16[256,32,384]{0,1,2:T(8,128)(2,1)}), bf16[256,32,384]{0,1,2:T(8,128)(2,1)}, u32[]{:S(2)}, u32[]{:S(2)}) async-start(bf16[256,32,384]{0,1,2:T(8,128)(2,1)} %copy.108), calls=%async_computation.2 | async-start | bytes 12582912 | tf_op jit(solution)/shard_map/all_to_all | solution.py:88
  122.3 0.5 all-gather.2.cloned.1.call-update
  122.9 0.2 all-reduce.2.cloned.1.call-start
  123.9 0.4 and.36
  124.3 1.7 copy.105
  126.0 75.4 %all-to-all-done.2 = bf16[256,32,384]{0,1,2:T(8,128)(2,1)} async-done(((bf16[256,32,384]{0,1,2:T(8,128)(2,1)}), bf16[256,32,384]{0,1,2:T(8,128)(2,1)}, u32[]{:S(2)}, u32[]{:S(2)}) %all-to-all-start.2) | async-done | bytes 6291488 | tf_op jit(solution)/shard_map/all_to_all | solution.py:88
  201.4 6.4 %copy.109 = bf16[256,32,384]{0,2,1:T(8,128)(2,1)S(1)} copy(bf16[256,32,384]{0,1,2:T(8,128)(2,1)} %all-to-all-done.2) | data formatting | bytes 12582912 | tf_op jit(solution)/shard_map/all_to_all | solution.py:88
  207.7 1.4 multiply_reduce_fusion
  209.2 10.5 %copy.110 = bf16[4,256,32,96]{1,0,3,2:T(4,128)(2,1)} copy(bf16[4,256,32,96]{1,2,3,0:T(8,128)(2,1)} %bitcast.14) | data formatting | bytes 12582912 | tf_op jit(solution)/shard_map/all_to_all | solution.py:88
  219.7 7.5 %copy.118 = bf16[384,8,4,256]{3,1,2,0:T(8,128)(2,1)} copy(bf16[384,8,4,256]{3,2,1,0:T(4,128)(2,1)} %bitcast.58) | data formatting | bytes 12582912
  227.2 9.8 %select_reduce_fusion = (f32[512]{0:T(512)S(1)}, f32[512,3072]{1,0:T(8,128)}) fusion(pred[512,3072]{1,0:T(32,128)(4,1)S(1)} %copy.105, pred[3072]{0:T(1024)(128)(4,1)S(1)} %get-tuple-element.104, f32[3072]{0:T(1024)S(1)} %mul.50, bf16[512,1024]{1,0:T(8,128)(2,1)} %all-gather.2.cloned.1.call-done, bf16[1024,3072]{0,1:T(8,128)(2,1)} %bitcast.61), kind=kOutput, calls=%fused_computation.20 | convolution fusion | flops 3229089280 | bytes 15221760 | tf_op jit(solution)/shard_map/while/body/eval_jaxpr/dot_general | solution.py:101
  237.0 6.5 %copy.112 = f32[512,3072]{0,1:T(8,128)} copy(f32[512,3072]{1,0:T(8,128)} %get-tuple-element.106) | data formatting | bytes 12582912 | tf_op jit(solution)/shard_map/while/body/eval_jaxpr/mul | solution.py:102
  243.5 8.9 %pmax.7 = f32[512]{0:T(512)S(1)} all-reduce(f32[512]{0:T(512)S(1)} %get-tuple-element.105), channel_id=1, replica_groups=mesh['cell'=8,'sub'=4] {'sub'}, use_global_device_ids=true, to_apply=%region_11.12 | all-reduce | flops 512 | bytes 4096 | tf_op jit(solution)/shard_map/pmax | solution.py:107
  252.3 5.5 %fusion.8 = f32[512,256,1]{1,0,2:T(8,128)} fusion(bf16[32,96,256]{2,1,0:T(8,128)(2,1)S(1)} %copy-done, f32[512,32,96]{0,2,1:T(8,128)} %bitcast.62, f32[512]{0:T(512)S(1)} %pmax.7, pred[32,96]{1,0:T(8,128)(4,1)S(1)} %broadcast_compare_fusion, pred[512,32]{0,1:T(8,128)(4,1)S(1)} %fusion.11), kind=kOutput, calls=%fused_computation.22 | convolution fusion | flops 811597824 | bytes 8410112 | tf_op jit(solution)/shard_map/while/body/eval_jaxpr/dot_general | solution.py:114
  257.9 4.5 %convert_reduce_fusion = f32[512]{0:T(512)S(1)} fusion(f32[512,3072]{1,0:T(8,128)} %get-tuple-element.106, pred[512,3072]{1,0:T(32,128)(4,1)S(1)} %copy.105, f32[512]{0:T(512)S(1)} %pmax.7, pred[3072]{0:T(1024)(128)(4,1)S(1)} %get-tuple-element.103), kind=kLoop, calls=%fused_computation.17 | loop fusion | flops 9436672 | bytes 7871488 | tf_op jit(solution)/shard_map/while/body/eval_jaxpr/reduce_sum | solution.py:113
  262.5 9.6 %psum.15 = f32[8,1,64]{2,1,0:T(1,128)} all-reduce(f32[8,1,64]{2,1,0:T(1,128)S(1)} %all_to_all.40), channel_id=1, replica_groups=mesh['cell'=8,'sub'=4] {'sub'}, use_global_device_ids=true, to_apply=%region_16.17 | all-reduce | flops 512 | bytes 4096 | tf_op jit(solution)/shard_map/psum | solution.py:120
  272.1 4.6 %all-to-all-start.5 = ((f32[8,1,64]{2,1,0:T(1,128)}), f32[8,1,64]{2,1,0:T(1,128)S(1)}, u32[]{:S(2)}, u32[]{:S(2)}) async-start(f32[8,1,64]{2,1,0:T(1,128)} %psum.15), calls=%async_computation.5 | async-start | bytes 8192 | tf_op jit(solution)/shard_map/all_to_all | solution.py:125
  276.8 5.4 %all-to-all-done.5 = f32[8,1,64]{2,1,0:T(1,128)S(1)} async-done(((f32[8,1,64]{2,1,0:T(1,128)}), f32[8,1,64]{2,1,0:T(1,128)S(1)}, u32[]{:S(2)}, u32[]{:S(2)}) %all-to-all-start.5) | async-done | bytes 2080 | tf_op jit(solution)/shard_map/all_to_all | solution.py:125
  282.2 7.9 %all_to_all.48 = f32[8,1,64]{2,1,0:T(1,128)S(1)} all-to-all(f32[8,1,64]{2,1,0:T(1,128)S(1)} %all_to_all.37), channel_id=1, replica_groups=mesh['cell'=8,'sub'=4] {'cell'}, dimensions={0} | all-to-all | bytes 4096 | tf_op jit(solution)/shard_map/all_to_all | solution.py:128
  290.1 13.5 %all-reduce.2.cloned.1.call-done = f32[8,64,256]{2,1,0:T(8,128)} async-done(((f32[8,64,256]{2,1,0:T(8,128)}), f32[8,64,256]{2,1,0:T(8,128)}) %all-reduce.2.cloned.1.call-update) | async-done | bytes 524304 | tf_op jit(solution)/shard_map/psum | solution.py:120
  303.6 4.6 %all-to-all-start.4 = ((f32[8,64,256]{2,1,0:T(8,128)}), f32[8,64,256]{2,1,0:T(8,128)S(1)}, u32[]{:S(2)}, u32[]{:S(2)}) async-start(f32[8,64,256]{2,1,0:T(8,128)} %all-reduce.2.cloned.1.call-done), calls=%async_computation.4 | async-start | bytes 1048576 | tf_op jit(solution)/shard_map/all_to_all | solution.py:122
  308.5 0.5 broadcast.152
  309.0 0.7 reduce.17
  309.8 3.5 %gather_fusion.2 = f32[512]{0:T(512)S(1)} fusion(f32[512]{0:T(512)S(1)} %reshape.231, s32[1024]{0:T(1024)S(1)} %pad_clamp_fusion), kind=kCustom, calls=%fused_computation.2 | custom fusion | bytes 6144 | tf_op jit(solution)/shard_map/gather | solution.py:54
  313.4 0.7 reduce.16
  314.1 3.5 %gather_fusion = f32[512]{0:T(512)S(1)} fusion(f32[512]{0:T(512)S(1)} %reshape.228, s32[1024]{0:T(1024)S(1)} %pad_clamp_fusion), kind=kCustom, calls=%fused_computation | custom fusion | bytes 6144 | tf_op jit(solution)/shard_map/gather | solution.py:53
  318.1 5.5 %all-to-all-done.4 = f32[8,64,256]{2,1,0:T(8,128)S(1)} async-done(((f32[8,64,256]{2,1,0:T(8,128)}), f32[8,64,256]{2,1,0:T(8,128)S(1)}, u32[]{:S(2)}, u32[]{:S(2)}) %all-to-all-start.4) | async-done | bytes 524320 | tf_op jit(solution)/shard_map/all_to_all | solution.py:122
  323.6 1.6 gather_fusion.1
  325.1 0.3 reshape.242
  325.5 0.7 multiply_reduce_fusion.1
  326.2 0.8 divide_convert_fusion
  (88 shorter events, 3.3 us)
Async XLA Ops:
  6.5 245.8 %copy-start = (bf16[32,96,256]{2,1,0:T(8,128)(2,1)S(1)}, bf16[32,96,256]{2,1,0:T(8,128)(2,1)}, u32[]{:S(2)}) copy-start(bf16[32,96,256]{2,1,0:T(8,128)(2,1)} %param.17) | copy-start | bytes 4718596
  13.4 79.5 %all-to-all-start = ((bf16[8,2,512]{2,1,0:T(2,128)(2,1)}), bf16[8,2,512]{2,1,0:T(2,128)(2,1)S(1)}, u32[]{:S(2)}, u32[]{:S(2)}) async-start(bf16[8,2,512]{2,1,0:T(2,128)(2,1)} %reshape.308), calls=%async_computation | async-start | bytes 32768 | tf_op jit(solution)/shard_map/all_to_all | solution.py:73
  21.1 57.1 %copy-start.4 = (bf16[32,256]{1,0:T(8,128)(2,1)S(1)}, bf16[32,256]{1,0:T(8,128)(2,1)}, u32[]{:S(2)}) copy-start(bf16[32,256]{1,0:T(8,128)(2,1)} %param.13) | copy-start | bytes 49156
  78.2 11.4 %copy-start.3 = (bf16[256,256]{1,0:T(8,128)(2,1)S(1)}, bf16[256,256]{1,0:T(8,128)(2,1)}, u32[]{:S(2)}) copy-start(bf16[256,256]{1,0:T(8,128)(2,1)} %param.10) | copy-start | bytes 393220
  92.9 23.3 %all-to-all-start.1 = ((bf16[8,64,256]{2,1,0:T(8,128)(2,1)}), bf16[8,64,256]{2,1,0:T(8,128)(2,1)S(1)}, u32[]{:S(2)}, u32[]{:S(2)}) async-start(bf16[8,64,256]{2,1,0:T(8,128)(2,1)} %bitcast.8), calls=%async_computation.1 | async-start | bytes 524288 | tf_op jit(solution)/shard_map/all_to_all | solution.py:70
  116.2 6.0 %copy-start.5 = (s32[32]{0:T(128)S(1)}, s32[32]{0:T(128)}, u32[]{:S(2)}) copy-start(s32[32]{0:T(128)} %param.16) | copy-start | bytes 388
  116.2 0.7 copy-start.2
  116.9 84.5 %all-to-all-start.2 = ((bf16[256,32,384]{0,1,2:T(8,128)(2,1)}), bf16[256,32,384]{0,1,2:T(8,128)(2,1)}, u32[]{:S(2)}, u32[]{:S(2)}) async-start(bf16[256,32,384]{0,1,2:T(8,128)(2,1)} %copy.108), calls=%async_computation.2 | async-start | bytes 12582912 | tf_op jit(solution)/shard_map/all_to_all | solution.py:88
  122.1 105.0 %all-gather.2.cloned.1.call-start = ((), (), s32[]{:S(2)}) async-start(), calls=%async_computation.6 | async-start | bytes 1310720 | tf_op jit(solution)/shard_map/all_gather | solution.py:81
  122.9 180.7 %all-reduce.2.cloned.1.call-start = ((), (), s32[]{:S(2)}) async-start(), calls=%async_computation.7 | async-start | bytes 1048576 | tf_op jit(solution)/shard_map/psum | solution.py:120
  272.1 10.1 %all-to-all-start.5 = ((f32[8,1,64]{2,1,0:T(1,128)}), f32[8,1,64]{2,1,0:T(1,128)S(1)}, u32[]{:S(2)}, u32[]{:S(2)}) async-start(f32[8,1,64]{2,1,0:T(1,128)} %psum.15), calls=%async_computation.5 | async-start | bytes 8192 | tf_op jit(solution)/shard_map/all_to_all | solution.py:125
  303.6 20.0 %all-to-all-start.4 = ((f32[8,64,256]{2,1,0:T(8,128)}), f32[8,64,256]{2,1,0:T(8,128)S(1)}, u32[]{:S(2)}, u32[]{:S(2)}) async-start(f32[8,64,256]{2,1,0:T(8,128)} %all-reduce.2.cloned.1.call-done), calls=%async_computation.4 | async-start | bytes 1048576 | tf_op jit(solution)/shard_map/all_to_all | solution.py:122
  314.1 12.8 %copy-start.1 = (bf16[32,96,256]{2,1,0:T(8,128)(2,1)S(1)}, bf16[32,96,256]{2,1,0:T(8,128)(2,1)}, u32[]{:S(2)}) copy-start(bf16[32,96,256]{2,1,0:T(8,128)(2,1)} %param.17) | copy-start | bytes 4718596
Sparse Core Ops, SparseCore 0:
  124.8 59.4 all-gather.1
  258.0 45.5 all-reduce.1
where the time goes:
time: 336 us; the launch traced here: 334 us
  waiting for transfers between devices  100 us (30%)
  local copies, waits for them, and re-layouts  73.6 us (22%)
  matrix products  72.1 us (21%)
  blocking collectives  26.4 us (8%)
  starting transfers between devices  26.2 us (8%)
  other arithmetic  21.5 us (6%)
  between operations  13.7 us (4%)
    all_to_all x1, waiting for transfers between devices, local(): lax.all_to_all(local_vectors, 'sub', split_axis=2, concat_axis=0, tiled=T...  75.4 us
    dot_general x16, matrix products, one_subspace(): return jnp.dot(book, onehot, preferred_element_type=jnp.float32)  56.8 us
    unnamed x17, local copies, waits for them, and re-layouts  21.7 us
    all_to_all x2, local copies, waits for them, and re-layouts, local(): lax.all_to_all(local_vectors, 'sub', split_axis=2, concat_axis=0, tiled=T...  16.9 us
    psum x1, waiting for transfers between devices, local(): part_sum, mass_sum = lax.psum((part, mass), 'sub')  13.5 us
    dot_general x1, matrix products, block_scores(): raw = jnp.dot(pair[0], decoded, preferred_element_type=jnp.float32)  9.78 us
    convert_element_type x1, local copies, waits for them, and re-layouts, decode(): (recon + coarse.T.astype(jnp.float32)[:, :, None]).astype(jnp.bfloat16)  9.6 us
    psum x1, blocking collectives, local(): part_sum, mass_sum = lax.psum((part, mass), 'sub')  9.6 us
  transfers between devices with their start and end apart: 7, of which 4 were waited for; matrix products, arithmetic and copies ran while one was open for 40% of the time, Pallas kernels for 0%

commit v1 on v0

v1 whole, which is shorter than its diff:
```python
import functools

import jax
import jax.numpy as jnp
from jax import lax
from jax.experimental import pallas as pl
from jax.experimental.pallas import tpu as pltpu
from jax.sharding import PartitionSpec as P

CAP = 64
LANES = 128
score_scale = 0.3
floor_score = -1e30
F32 = jnp.float32
BF16 = jnp.bfloat16


def iota(shape, dim):
    return lax.broadcasted_iota(jnp.int32, shape, dim)


def positions(meta_ref, groups):
    count = meta_ref.shape[1]
    padded = -(-groups // 8) * 8
    group_ids = iota((padded, count), 0)
    first = (meta_ref[0:1, :] == group_ids).astype(F32)
    second = (meta_ref[1:2, :] == group_ids).astype(F32)
    routed = first + second
    before = (iota((count, count), 0) < iota((count, count), 1)).astype(F32).astype(BF16)
    earlier = jnp.dot(routed.astype(BF16), before, preferred_element_type=F32)
    return first, second, routed, earlier


def pack_kernel(groups, half, meta_ref, rows_ref, buffer_ref, away_ref):
    count = meta_ref.shape[1]
    first, second, routed, earlier = positions(meta_ref, groups)
    spot = routed * (earlier + 1.0) - 1.0
    cell_ids = iota((LANES, count), 0)

    def named(start):
        marks = jnp.zeros((LANES, count), F32)
        for k in range(half):
            marks += (meta_ref[start + k : start + k + 1, :] == cell_ids).astype(F32)
        return marks

    named_first, named_second = named(2), named(2 + half)
    ranks = iota((CAP, count), 0).astype(F32)
    for g in range(groups):
        onehot = (ranks == spot[g : g + 1, :]).astype(F32).astype(BF16)
        buffer_ref[g * CAP : (g + 1) * CAP, :] = jnp.dot(
            onehot, rows_ref[...], preferred_element_type=F32
        ).astype(BF16)
        marks = first[g : g + 1, :] * named_first + second[g : g + 1, :] * named_second
        there = lax.dot_general(
            onehot, marks.astype(BF16), (((1,), (1,)), ((), ())), preferred_element_type=F32
        )
        away_ref[g * CAP : (g + 1) * CAP, :] = (1.0 - there).astype(BF16)


def score_kernel(
    row_local,
    codes_ref,
    books_ref,
    coarse_ref,
    lengths_ref,
    queries_ref,
    away_ref,
    values_ref,
    peak_ref,
    ids,
    vectors,
    squares,
    best,
):
    subs, rows = codes_ref.shape
    width = books_ref.shape[1]
    cells = coarse_ref.shape[0]
    blocks = rows // LANES
    ids[...] = codes_ref[...].astype(F32).astype(jnp.int32)
    offset = iota((cells, rows), 1) - iota((cells, rows), 0) * row_local
    inside = (offset >= 0) & (offset < row_local)
    spread = inside.astype(F32).astype(BF16)
    vectors[...] = lax.dot_general(
        coarse_ref[...], spread, (((0,), (0,)), ((), ())), preferred_element_type=F32
    ).astype(BF16)
    squares[...] = jnp.zeros_like(squares)

    @pl.loop(0, subs // 8)
    def _(group):
        for j in range(8):
            m = group * 8 + j
            book = books_ref[m].astype(F32)
            low, high = book[:, :LANES], book[:, LANES:]
            place = pl.ds(pl.multiple_of(m * width, width), width)
            for b in range(blocks):
                lanes = slice(b * LANES, (b + 1) * LANES)
                near = ids[pl.ds(pl.multiple_of(group * 8, 8), 8), lanes]
                code = jnp.broadcast_to(near[j : j + 1, :], (width, LANES))
                index = code & (LANES - 1)
                picked = jnp.where(
                    code < LANES,
                    jnp.take_along_axis(low, index, axis=1, mode="promise_in_bounds"),
                    jnp.take_along_axis(high, index, axis=1, mode="promise_in_bounds"),
                )
                summed = (picked + vectors[place, lanes].astype(F32)).astype(BF16)
                vectors[place, lanes] = summed
                back = summed.astype(F32)
                back = back * back
                squares[:, lanes] += back[:8] + back[8:]

    first_row = lax.axis_index("sub") * row_local
    live = jnp.sum(
        (inside & (offset + first_row < lengths_ref[...])).astype(F32), axis=0, keepdims=True
    )
    half_norm = 0.5 * jnp.sum(squares[...], axis=0, keepdims=True)
    squares[0:1, :] = jnp.where(live > 0.5, half_norm, -floor_score)
    step = 512 if rows % 512 == 0 else 256
    best[...] = jnp.full_like(best, 3.0 * floor_score)

    @pl.loop(0, rows // step)
    def _(n):
        lanes = pl.ds(pl.multiple_of(n * step, step), step)
        raw = jnp.dot(queries_ref[...], vectors[:, lanes], preferred_element_type=F32)
        shift = iota((LANES, step), 1) + n * step - iota((LANES, step), 0) * row_local
        far = jnp.where((shift >= 0) & (shift < row_local), floor_score, 0.0).astype(BF16)
        raw = raw + jnp.dot(away_ref[...], far, preferred_element_type=F32)
        values = (raw - squares[0:1, lanes]) * score_scale
        values_ref[:, lanes] = values
        top = best[...]
        for b in range(step // LANES):
            top = jnp.maximum(top, values[:, b * LANES : (b + 1) * LANES])
        best[...] = top

    peak_ref[...] = jnp.max(best[...], axis=1, keepdims=True)


def sum_kernel(values_ref, peak_ref, payload_ref, sums_ref):
    total = values_ref.shape[0]
    width = payload_ref.shape[1]
    block = 64

    @pl.loop(0, total // block)
    def _(n):
        place = pl.ds(pl.multiple_of(n * block, block), block)
        peak = peak_ref[place, :]
        weights = jnp.exp(values_ref[place, :] - peak).astype(BF16)
        mass = jnp.sum(weights.astype(F32), axis=1, keepdims=True)
        sums_ref[place, :width] = jnp.dot(weights, payload_ref[...], preferred_element_type=F32)
        lane = iota((block, LANES), 1)
        mine = (lax.axis_index("sub") == 0).astype(F32)
        sums_ref[place, width:] = jnp.where(
            lane == 0, mass, jnp.where(lane == 1, peak * mine, 0.0)
        )


def combine_kernel(groups, meta_ref, back_ref, pooled_ref):
    count = meta_ref.shape[1]
    total, wide = back_ref.shape
    width = wide - LANES
    first, second, _, earlier = positions(meta_ref, groups)

    def gathered(route, marks):
        spot = jnp.sum(marks * earlier, axis=0, keepdims=True).astype(jnp.int32)
        slot = meta_ref[route : route + 1, :] * CAP + spot
        onehot = (iota((total, count), 0) == slot).astype(F32).astype(BF16)

        def pick(part):
            return lax.dot_general(
                onehot, part, (((0,), (0,)), ((), ())), preferred_element_type=F32
            )

        sums = back_ref[...]
        out = jnp.zeros((count, wide), F32)
        for _ in range(3):
            piece = sums.astype(BF16)
            out = out + pick(piece)
            sums = sums - piece.astype(F32)
        return out[:, :width], out[:, width : width + 1], out[:, width + 1 : width + 2]

    part_0, mass_0, peak_0 = gathered(0, first)
    part_1, mass_1, peak_1 = gathered(1, second)
    top = jnp.maximum(peak_0, peak_1)
    scale_0, scale_1 = jnp.exp(peak_0 - top), jnp.exp(peak_1 - top)
    lower = scale_0 * mass_0 + scale_1 * mass_1
    pooled_ref[...] = ((scale_0 * part_0 + scale_1 * part_1) / lower).astype(BF16)


def call(kernel, outs, *args, scratch=()):
    spec = pl.BlockSpec(memory_space=pltpu.VMEM)
    return pl.pallas_call(
        kernel,
        out_shape=[jax.ShapeDtypeStruct(shape, dtype) for shape, dtype in outs],
        in_specs=[spec] * len(args),
        out_specs=[spec] * len(outs),
        scratch_shapes=list(scratch),
        compiler_params=pltpu.CompilerParams(vmem_limit_bytes=48 * 1024 * 1024),
    )(*args)


def local(queries, probe_groups, probe_cells, coarse, codebooks, codes, lengths, payload):
    groups, shares = lax.axis_size("cell"), lax.axis_size("sub")
    count, own_width = queries.shape
    half = probe_cells.shape[2]
    cells, own_subs, row_slots = codes.shape
    row_local = row_slots // shares
    rows = cells * row_local
    total = groups * CAP
    width = payload.shape[2]
    meta = jnp.concatenate([probe_groups, probe_cells.reshape(count, -1)], axis=1).T

    sent_codes = jnp.transpose(
        codes.astype(BF16).reshape(cells, own_subs, shares, row_local), (2, 1, 0, 3)
    ).reshape(shares, own_subs, rows)
    all_codes = lax.all_to_all(sent_codes, "sub", split_axis=0, concat_axis=0, tiled=True)
    all_codes = all_codes.reshape(shares * own_subs, rows)
    books = lax.all_gather(codebooks, "sub", axis=0, tiled=True)
    centers = lax.all_gather(coarse, "sub", axis=1, tiled=True)

    buffer, away = call(
        functools.partial(pack_kernel, groups, half),
        [((total, own_width), BF16), ((total, LANES), BF16)],
        meta,
        queries,
    )

    def swap(array):
        shape = array.shape
        return lax.all_to_all(
            array.reshape(groups, shape[0] // groups, shape[1]),
            "cell",
            split_axis=0,
            concat_axis=0,
            tiled=True,
        ).reshape(shape)

    buffer, away = swap(buffer), swap(away)
    full_rows = lax.all_gather(buffer, "sub", axis=1, tiled=True)

    values, peak = call(
        functools.partial(score_kernel, row_local),
        [((total, rows), F32), ((total, 1), F32)],
        all_codes,
        books,
        centers,
        lengths.reshape(cells, 1),
        full_rows,
        away,
        scratch=(
            pltpu.VMEM(all_codes.shape, jnp.int32),
            pltpu.VMEM((centers.shape[1], rows), BF16),
            pltpu.VMEM((8, rows), F32),
            pltpu.VMEM((total, LANES), F32),
        ),
    )
    peak = lax.pmax(peak, "sub")
    (sums,) = call(
        sum_kernel,
        [((total, width + LANES), F32)],
        values,
        peak,
        payload.reshape(rows, width),
    )
    wide = width + LANES
    shared = lax.psum_scatter(
        sums.reshape(groups, CAP, wide), "sub", scatter_dimension=1, tiled=True
    )
    back = lax.all_to_all(shared, "cell", split_axis=0, concat_axis=0, tiled=True)
    back = lax.all_gather(back, "sub", axis=1, tiled=True).reshape(total, wide)
    (pooled,) = call(
        functools.partial(combine_kernel, groups), [((count, width), BF16)], meta, back
    )
    return pooled


def solution(mesh):
    placed = (
        P("cell", "sub"),
        P("cell", None),
        P("cell", None, None),
        P("cell", "sub"),
        P("sub", None, None),
        P("cell", "sub", None),
        P("cell"),
        P("cell", "sub", None),
    )
    return jax.shard_map(
        local, mesh=mesh, in_specs=placed, out_specs=P("cell", None), check_vma=False
    )
```

time: 336 us -> 166 us (0.49)
  waiting for transfers between devices: 100 us -> 27.8 us
  matrix products: 72.1 us -> 0 us
  local copies, waits for them, and re-layouts: 73.6 us -> 5.05 us
  blocking collectives: 26.4 us -> 80.3 us
  Pallas kernels: 0 us -> 29.2 us
  other arithmetic: 21.5 us -> 2.07 us
  starting transfers between devices: 26.2 us -> 7.11 us
    all_to_all x5 -> x2, waiting for transfers between devices: 86.3 us -> 3.32 us  [the longest x1 3.31 us: swap(): lax.all_to_all(array.reshape(groups, shape[0] // groups, shape[1]), 'cell...]
    dot_general x18 -> x0, matrix products: 72.1 us -> none  [the longest x16 56.8 us: one_subspace(): return jnp.dot(book, onehot, preferred_element_type=jnp.float32)]
    all_gather x0 -> x3, blocking collectives: none -> 31.9 us  [the longest x1 12.1 us: local(): back = lax.all_gather(back, 'sub', axis=1, tiled=True).reshape(total, wide)]
    pallas_call x0 -> x4, Pallas kernels: none -> 29.2 us  [call(): pl.pallas_call(kernel, out_shape=[jax.ShapeDtypeStruct(shape, dtype) for...]
    reduce_scatter x0 -> x1, waiting for transfers between devices: none -> 24.4 us  [local(): lax.psum_scatter(sums.reshape(groups, CAP, wide), 'sub', scatter_dimensio...]
    all_to_all x1 -> x2, blocking collectives: 7.91 us -> 28.9 us  [the longest x1 16 us: swap(): lax.all_to_all(array.reshape(groups, shape[0] // groups, shape[1]), 'cell...]
    unnamed x17 -> x6, local copies, waits for them, and re-layouts: 21.7 us -> 2.12 us
    all_to_all x5 -> x2, starting transfers between devices: 25.9 us -> 7.1 us  [the longest x1 3.72 us: local(): lax.all_to_all(sent_codes, 'sub', split_axis=0, concat_axis=0, tiled=True)]
  transfers between devices with their start and end apart: 7 -> 4, of which waited for: 4 -> 2; matrix products, arithmetic and copies ran while one was open for 40% -> 2% of each run, Pallas kernels for 0% -> 0%
where the time goes in v1:
time: 166 us; the launch traced here: 165 us
  blocking collectives  80.3 us (48%)
  Pallas kernels  29.2 us (18%)
  waiting for transfers between devices  27.8 us (17%)
  between operations  13.5 us (8%)
  starting transfers between devices  7.11 us (4%)
  local copies, waits for them, and re-layouts  5.05 us (3%)
  other arithmetic  2.07 us (1%)
    pallas_call x4, Pallas kernels, call(): pl.pallas_call(kernel, out_shape=[jax.ShapeDtypeStruct(shape, dtype) for...  29.2 us
    reduce_scatter x1, waiting for transfers between devices, local(): lax.psum_scatter(sums.reshape(groups, CAP, wide), 'sub', scatter_dimensio...  24.4 us
    pmax x1, blocking collectives, local(): peak = lax.pmax(peak, 'sub')  19.5 us
    all_to_all x1, blocking collectives, swap(): lax.all_to_all(array.reshape(groups, shape[0] // groups, shape[1]), 'cell...  16 us
    all_to_all x1, blocking collectives, local(): lax.all_to_all(shared, 'cell', split_axis=0, concat_axis=0, tiled=True)  13 us
    all_gather x1, blocking collectives, local(): back = lax.all_gather(back, 'sub', axis=1, tiled=True).reshape(total, wide)  12.1 us
    all_gather x1, blocking collectives, local(): centers = lax.all_gather(coarse, 'sub', axis=1, tiled=True)  10.3 us
    all_gather x1, blocking collectives, local(): books = lax.all_gather(codebooks, 'sub', axis=0, tiled=True)  9.64 us
  transfers between devices with their start and end apart: 4, of which 2 were waited for; matrix products, arithmetic and copies ran while one was open for 2% of the time, Pallas kernels for 0%

profile of v1, /device:TPU:0, one launch (start us, length us, event | category | flops | bytes accessed | tf_op | source)
XLA Modules:
  0.0 165.0 jit_solution(15683577320406186313)
XLA Ops:
  6.5 0.0 copy-start
  6.5 0.0 all-gather.2.cloned.1.call-start
  6.5 0.9 add_bitcast_fusion.meta_ref
  7.4 0.0 copy-start.2
  7.4 0.9 copy-done.2
  8.3 1.7 %shard_map.82 = (bf16[512,256]{1,0:T(8,128)(2,1)S(1)}, bf16[512,128]{1,0:T(8,128)(2,1)}) custom-call(s32[34,256]{1,0:T(8,128)S(1)} %add_bitcast_fusion.meta_ref, bf16[256,256]{1,0:T(8,128)(2,1)S(1)} %copy-done.2), custom_call_target="tpu_custom_call" | custom-call | tf_op jit(solution)/shard_map/pallas_call | solution.py:190
  10.0 16.0 %all_to_all.20 = bf16[8,64,256]{2,1,0:T(8,128)(2,1)} all-to-all(bf16[8,64,256]{2,1,0:T(8,128)(2,1)S(1)} %bitcast.19), channel_id=1, replica_groups=mesh['cell'=8,'sub'=4] {'cell'}, dimensions={0} | all-to-all | bytes 524288 | tf_op jit(solution)/shard_map/all_to_all | solution.py:228
  26.0 0.0 all-gather.2.cloned.1.call-update
  26.0 3.4 %all-to-all-start.2 = ((bf16[8,64,128]{2,1,0:T(8,128)(2,1)}), bf16[8,64,128]{2,1,0:T(8,128)(2,1)S(1)}, u32[]{:S(2)}, u32[]{:S(2)}) async-start(bf16[8,64,128]{2,1,0:T(8,128)(2,1)} %bitcast.7), calls=%async_computation.2 | async-start | bytes 262144 | tf_op jit(solution)/shard_map/all_to_all | solution.py:228
  29.4 1.2 convert_element_type.3
  30.6 0.4 reshape.37
  30.9 0.3 copy.11
  31.3 1.5 reshape.38
  32.8 3.3 %all-to-all-done.2 = bf16[8,64,128]{2,1,0:T(8,128)(2,1)S(1)} async-done(((bf16[8,64,128]{2,1,0:T(8,128)(2,1)}), bf16[8,64,128]{2,1,0:T(8,128)(2,1)S(1)}, u32[]{:S(2)}, u32[]{:S(2)}) %all-to-all-start.2) | async-done | bytes 131104 | tf_op jit(solution)/shard_map/all_to_all | solution.py:228
  36.1 3.7 %all-to-all-start = ((bf16[4,16,3072]{2,1,0:T(8,128)(2,1)}), bf16[4,16,3072]{2,1,0:T(8,128)(2,1)S(1)}, u32[]{:S(2)}, u32[]{:S(2)}) async-start(bf16[4,16,3072]{2,1,0:T(8,128)(2,1)} %reshape.38), calls=%async_computation | async-start | bytes 786432 | tf_op jit(solution)/shard_map/all_to_all | solution.py:214
  39.8 0.0 reduce-scatter.2.cloned.1.call-start
  39.8 0.7 copy.12.lengths_ref
  40.5 10.3 %all_gather.13.coarse_ref = bf16[32,1024]{1,0:T(8,128)(2,1)S(1)} all-gather(bf16[32,256]{1,0:T(8,128)(2,1)} %param.11), channel_id=1, replica_groups=mesh['cell'=8,'sub'=4] {'sub'}, dimensions={1}, use_global_device_ids=true | all-gather | bytes 81920 | tf_op jit(solution)/shard_map/all_gather | solution.py:217
  50.8 9.6 %all_gather.12.books_ref = bf16[64,16,256]{2,1,0:T(8,128)(2,1)S(1)} all-gather(bf16[16,16,256]{2,1,0:T(8,128)(2,1)} %param.12), channel_id=1, replica_groups=mesh['cell'=8,'sub'=4] {'sub'}, dimensions={0}, use_global_device_ids=true | all-gather | bytes 655360 | tf_op jit(solution)/shard_map/all_gather | solution.py:216
  60.4 0.0 all-to-all-done
  60.4 0.0 all-gather.2.cloned.1.call-done.queries_ref
  60.5 0.0 copy-start.1
  60.5 1.2 copy-done.1
  61.7 18.1 %shard_map.83 = (f32[512,3072]{1,0:T(8,128)}, f32[512,1]{1,0:T(8,128)S(1)}) custom-call(bf16[64,3072]{1,0:T(8,128)(2,1)S(1)} %bitcast.16, bf16[64,16,256]{2,1,0:T(8,128)(2,1)S(1)} %all_gather.12.books_ref, bf16[32,1024]{1,0:T(8,128)(2,1)S(1)} %all_gather.13.coarse_ref, s32[32,1]{1,0:T(8,128)S(1)} %copy.12.lengths_ref, bf16[512,1024]{1,0:T(8,128)(2,1)S(1)} %copy-done.1, ...), custom_call_target="tpu_custom_call" | custom-call | tf_op jit(solution)/shard_map/pallas_call | solution.py:190
  79.8 19.5 %pmax.7.peak_ref = f32[512,1]{1,0:T(8,128)S(1)} all-reduce(f32[512,1]{1,0:T(8,128)S(1)} %get-tuple-element.12), channel_id=1, replica_groups=mesh['cell'=8,'sub'=4] {'sub'}, use_global_device_ids=true, to_apply=%region_0.0 | all-reduce | flops 512 | bytes 4096 | tf_op jit(solution)/shard_map/pmax | solution.py:255
  99.3 0.0 copy-done
  99.3 7.4 %shard_map.84 = f32[512,384]{1,0:T(8,128)} custom-call(f32[512,3072]{1,0:T(8,128)} %get-tuple-element.11.values_ref, f32[512,1]{1,0:T(8,128)S(1)} %pmax.7.peak_ref, bf16[3072,256]{1,0:T(8,128)(2,1)S(1)} %bitcast.17), custom_call_target="tpu_custom_call" | custom-call | tf_op jit(solution)/shard_map/pallas_call | solution.py:190
  106.7 0.0 reduce-scatter.2.cloned.1.call-update
  106.7 24.4 %reduce-scatter.2.cloned.1.call-done = f32[8,16,384]{2,1,0:T(8,128)} async-done(((f32[8,64,384]{2,1,0:T(8,128)}), f32[8,16,384]{2,1,0:T(8,128)}) %reduce-scatter.2.cloned.1.call-update) | async-done | bytes 196624 | tf_op jit(solution)/shard_map/reduce_scatter | solution.py:264
  131.1 13.0 %all_to_all.21 = f32[8,16,384]{2,1,0:T(8,128)S(1)} all-to-all(f32[8,16,384]{2,1,0:T(8,128)} %reduce-scatter.2.cloned.1.call-done), channel_id=1, replica_groups=mesh['cell'=8,'sub'=4] {'cell'}, dimensions={0} | all-to-all | bytes 393216 | tf_op jit(solution)/shard_map/all_to_all | solution.py:267
  144.1 12.1 %all_gather.15 = f32[8,64,384]{2,1,0:T(8,128)S(1)} all-gather(f32[8,16,384]{2,1,0:T(8,128)S(1)} %all_to_all.21), channel_id=1, replica_groups=mesh['cell'=8,'sub'=4] {'sub'}, dimensions={1}, use_global_device_ids=true | all-gather | bytes 983040 | tf_op jit(solution)/shard_map/all_gather | solution.py:268
  156.1 2.0 %shard_map.85 = bf16[256,256]{1,0:T(8,128)(2,1)} custom-call(s32[34,256]{1,0:T(8,128)S(1)} %add_bitcast_fusion.meta_ref, f32[512,384]{1,0:T(8,128)S(1)} %bitcast.15), custom_call_target="tpu_custom_call" | custom-call | tf_op jit(solution)/shard_map/pallas_call | solution.py:190
Async XLA Ops:
  6.5 92.8 %copy-start = (bf16[32,96,256]{2,1,0:T(8,128)(2,1)S(1)}, bf16[32,96,256]{2,1,0:T(8,128)(2,1)}, u32[]{:S(2)}) copy-start(bf16[32,96,256]{2,1,0:T(8,128)(2,1)} %param.15) | copy-start | bytes 4718596
  6.5 53.9 %all-gather.2.cloned.1.call-start = ((), (), s32[]{:S(2)}) async-start(), calls=%async_computation.5 | async-start | bytes 1310720 | tf_op jit(solution)/shard_map/all_gather | solution.py:237
  7.4 0.9 copy-start.2
  26.0 10.1 %all-to-all-start.2 = ((bf16[8,64,128]{2,1,0:T(8,128)(2,1)}), bf16[8,64,128]{2,1,0:T(8,128)(2,1)S(1)}, u32[]{:S(2)}, u32[]{:S(2)}) async-start(bf16[8,64,128]{2,1,0:T(8,128)(2,1)} %bitcast.7), calls=%async_computation.2 | async-start | bytes 262144 | tf_op jit(solution)/shard_map/all_to_all | solution.py:228
  36.1 24.4 %all-to-all-start = ((bf16[4,16,3072]{2,1,0:T(8,128)(2,1)}), bf16[4,16,3072]{2,1,0:T(8,128)(2,1)S(1)}, u32[]{:S(2)}, u32[]{:S(2)}) async-start(bf16[4,16,3072]{2,1,0:T(8,128)(2,1)} %reshape.38), calls=%async_computation | async-start | bytes 786432 | tf_op jit(solution)/shard_map/all_to_all | solution.py:214
  39.8 91.3 %reduce-scatter.2.cloned.1.call-start = ((), (), s32[]{:S(2)}) async-start(), calls=%async_computation.6 | async-start | bytes 983040 | tf_op jit(solution)/shard_map/reduce_scatter | solution.py:264
  60.5 1.2 copy-start.1
Sparse Core Ops, SparseCore 0:
  26.1 26.5 all-gather.1
  106.8 24.2 reduce-scatter.1

commit v2 on v1

v2 whole, which is shorter than its diff:
```python
import functools

import jax
import jax.numpy as jnp
from jax import lax
from jax.experimental import pallas as pl
from jax.experimental.pallas import tpu as pltpu
from jax.sharding import PartitionSpec as P

CAP = 64
LANES = 128
score_scale = 0.3
floor_score = -1e30
F32 = jnp.float32
BF16 = jnp.bfloat16


def iota(shape, dim):
    return lax.broadcasted_iota(jnp.int32, shape, dim)


def positions(meta_ref, groups):
    count = meta_ref.shape[1]
    padded = -(-groups // 8) * 8
    group_ids = iota((padded, count), 0)
    first = (meta_ref[0:1, :] == group_ids).astype(F32)
    second = (meta_ref[1:2, :] == group_ids).astype(F32)
    routed = first + second
    before = (iota((count, count), 0) < iota((count, count), 1)).astype(F32).astype(BF16)
    earlier = jnp.dot(routed.astype(BF16), before, preferred_element_type=F32)
    return first, second, routed, earlier


def pack_kernel(groups, half, meta_ref, rows_ref, buffer_ref, away_ref):
    count = meta_ref.shape[1]
    first, second, routed, earlier = positions(meta_ref, groups)
    spot = routed * (earlier + 1.0) - 1.0
    cell_ids = iota((LANES, count), 0)

    def named(start):
        marks = jnp.zeros((LANES, count), F32)
        for k in range(half):
            marks += (meta_ref[start + k : start + k + 1, :] == cell_ids).astype(F32)
        return marks

    named_first, named_second = named(2), named(2 + half)
    ranks = iota((CAP, count), 0).astype(F32)
    for g in range(groups):
        onehot = (ranks == spot[g : g + 1, :]).astype(F32).astype(BF16)
        buffer_ref[g] = jnp.dot(
            onehot, rows_ref[...], preferred_element_type=F32
        ).astype(BF16)
        marks = first[g : g + 1, :] * named_first + second[g : g + 1, :] * named_second
        there = lax.dot_general(
            onehot, marks.astype(BF16), (((1,), (1,)), ((), ())), preferred_element_type=F32
        )
        away_ref[g] = (1.0 - there).astype(BF16)


def decode_share(subs, width, blocks, codes_ref, books_ref, base, ids, vectors, squares):
    near = min(8, subs)
    ids[...] = codes_ref[...].astype(F32).astype(jnp.int32)

    def some(start):
        @pl.loop(0, blocks // 2)
        def _(pair):
            for u in range(2):
                lanes = pl.ds(pl.multiple_of(pair * (2 * LANES) + u * LANES, LANES), LANES)
                held = ids[pl.ds(start, near), lanes]
                total = jnp.zeros((8, LANES), F32)
                for j in range(near):
                    book = books_ref[start + j].astype(F32)
                    code = jnp.broadcast_to(held[j : j + 1, :], (width, LANES))
                    index = code & (LANES - 1)
                    picked = jnp.where(
                        code < LANES,
                        jnp.take_along_axis(book[:, :LANES], index, axis=1, mode="promise_in_bounds"),
                        jnp.take_along_axis(book[:, LANES:], index, axis=1, mode="promise_in_bounds"),
                    )
                    place = pl.ds(pl.multiple_of(base + (start + j) * width, width), width)
                    summed = (picked + vectors[place, lanes].astype(F32)).astype(BF16)
                    vectors[place, lanes] = summed
                    back = summed.astype(F32)
                    back = back * back
                    total += back[:8] + back[8:]
                squares[:, lanes] += total

    if subs == near:
        some(0)
    else:

        @pl.loop(0, subs // near)
        def _(group):
            some(pl.multiple_of(group * near, near))


def whole_kernel(
    groups,
    shares,
    half,
    row_local,
    fold,
    meta_ref,
    rows_ref,
    codes_ref,
    books_ref,
    coarse_ref,
    lengths_ref,
    payload_ref,
    pooled_ref,
    buffer,
    away_out,
    queries,
    away,
    codes_in,
    books_in,
    coarse_in,
    ids,
    vectors,
    squares,
    best,
    values,
    peak_row,
    part,
    masses,
    mass_row,
    share_out,
    share_in,
    back_out,
    back_in,
    stat_out,
    stat_in,
    columns,
    send_sem,
    recv_sem,
):
    me_cell, me_sub = lax.axis_index("cell"), lax.axis_index("sub")
    count = meta_ref.shape[1]
    subs, rows = ids.shape
    book_width = books_ref.shape[1]
    cells, own_width = coarse_ref.shape
    total = groups * CAP
    width = payload_ref.shape[1]
    own_columns = width // shares
    short = CAP // fold
    blocks = rows // LANES
    step = 512 if rows % 512 == 0 else 256
    used = [0]

    def device(cell_off, sub_off):
        return (lax.rem(me_cell + cell_off, groups), lax.rem(me_sub + sub_off, shares))

    def send(src, dst, cell_off, sub_off):
        i = used[0]
        used[0] += 1
        copy = pltpu.make_async_remote_copy(
            src_ref=src,
            dst_ref=dst,
            send_sem=send_sem.at[i],
            recv_sem=recv_sem.at[i],
            device_id=device(cell_off, sub_off),
            device_id_type=pl.DeviceIdType.MESH,
        )
        copy.start()
        return copy

    barrier = pltpu.get_barrier_semaphore()
    for off in range(1, groups):
        pl.semaphore_signal(
            barrier, inc=1, device_id=device(off, 0), device_id_type=pl.DeviceIdType.MESH
        )
    for off in range(1, shares):
        pl.semaphore_signal(
            barrier, inc=1, device_id=device(0, off), device_id_type=pl.DeviceIdType.MESH
        )
    pl.semaphore_wait(barrier, groups + shares - 2)

    everything = []
    lists = [None]
    for off in range(1, shares):
        target = lax.rem(me_sub + off, shares)
        lists.append(
            [
                send(codes_ref.at[target], codes_in.at[off - 1], 0, off),
                send(books_ref, books_in.at[off - 1], 0, off),
                send(coarse_ref, coarse_in.at[off - 1], 0, off),
            ]
        )
        everything += lists[-1]

    pack_kernel(groups, half, meta_ref, rows_ref, buffer, away_out)
    routed = [None]
    for off in range(1, groups):
        target = lax.rem(me_cell + off, groups)
        routed.append(
            [
                send(buffer.at[target], queries.at[0, me_cell], off, 0),
                send(away_out.at[target], away.at[me_cell], off, 0),
            ]
        )
        everything += routed[-1]
    queries[0, me_cell] = buffer[me_cell]
    away[me_cell] = away_out[me_cell]
    spread_out = []

    def forward(off):
        if off:
            for copy in routed[off]:
                copy.wait_recv()
        source = lax.rem(me_cell + groups - off, groups)
        for sub_off in range(1, shares):
            spread_out.append(
                send(queries.at[0, source], queries.at[sub_off, source], 0, sub_off)
            )

    forward(0)
    squares[...] = jnp.zeros_like(squares)
    passed = 1
    for k in range(shares):
        if k:
            for copy in lists[k]:
                copy.wait_recv()
        centers = coarse_in.at[k - 1] if k else coarse_ref

        @pl.loop(0, rows // step)
        def _(n):
            lanes = pl.ds(pl.multiple_of(n * step, step), step)
            shift = iota((cells, step), 1) + n * step - iota((cells, step), 0) * row_local
            inside = ((shift >= 0) & (shift < row_local)).astype(F32).astype(BF16)
            vectors[k * own_width : (k + 1) * own_width, lanes] = lax.dot_general(
                centers[...], inside, (((0,), (0,)), ((), ())), preferred_element_type=F32
            ).astype(BF16)

        decode_share(
            subs,
            book_width,
            blocks,
            codes_in.at[k - 1] if k else codes_ref.at[me_sub],
            books_in.at[k - 1] if k else books_ref,
            k * own_width,
            ids,
            vectors,
            squares,
        )
        until = min(groups, 1 + -(-(groups - 1) * (k + 1) // min(shares, 2)))
        for off in range(passed, until):
            forward(off)
        passed = max(passed, until)
    everything += spread_out

    offset = iota((cells, rows), 1) - iota((cells, rows), 0) * row_local
    inside = (offset >= 0) & (offset < row_local)
    live = jnp.sum(
        (inside & (offset + me_sub * row_local < lengths_ref[...])).astype(F32),
        axis=0,
        keepdims=True,
    )
    half_norm = 0.5 * jnp.sum(squares[...], axis=0, keepdims=True)
    squares[0:1, :] = jnp.where(live > 0.5, half_norm, -floor_score)
    best[...] = jnp.full_like(best, 3.0 * floor_score)
    for copy in spread_out:
        copy.wait_recv()

    @pl.loop(0, rows // step)
    def _(n):
        lanes = pl.ds(pl.multiple_of(n * step, step), step)
        shift = iota((LANES, step), 1) + n * step - iota((LANES, step), 0) * row_local
        far = jnp.where((shift >= 0) & (shift < row_local), floor_score, 0.0).astype(BF16)
        raw = jnp.dot(away[...].reshape(total, LANES), far, preferred_element_type=F32)
        for k in range(shares):
            raw = raw + jnp.dot(
                queries[k].reshape(total, own_width),
                vectors[k * own_width : (k + 1) * own_width, lanes],
                preferred_element_type=F32,
            )
        scores = (raw - squares[0:1, lanes]) * score_scale
        values[:, lanes] = scores
        top = best[...]
        for b in range(step // LANES):
            top = jnp.maximum(top, scores[:, b * LANES : (b + 1) * LANES])
        best[...] = top

    peak_row[0] = jnp.broadcast_to(
        jnp.max(jnp.transpose(best[...]), axis=0, keepdims=True), (8, total)
    )
    tops = [send(peak_row.at[0], peak_row.at[off], 0, off) for off in range(1, shares)]
    everything += tops
    for copy in tops:
        copy.wait_recv()
    peak = jnp.max(peak_row[...], axis=0)
    best[...] = jnp.transpose(jnp.broadcast_to(peak[0:1], (LANES, total)))
    part[...] = jnp.zeros_like(part)
    masses[...] = jnp.zeros_like(masses)

    @pl.loop(0, rows // step)
    def _(n):
        lanes = pl.ds(pl.multiple_of(n * step, step), step)
        mass = masses[...]
        pieces = []
        for b in range(step // LANES):
            inner = pl.ds(pl.multiple_of(n * step + b * LANES, LANES), LANES)
            piece = jnp.exp(values[:, inner] - best[...]).astype(BF16)
            mass = mass + piece.astype(F32)
            pieces.append(piece)
        masses[...] = mass
        part[...] += jnp.dot(
            jnp.concatenate(pieces, axis=1), payload_ref[lanes, :], preferred_element_type=F32
        )

    mass_row[0] = jnp.broadcast_to(
        jnp.sum(jnp.transpose(masses[...]), axis=0, keepdims=True), (8, total)
    )
    sums = part[...].reshape(groups, CAP, width)
    for t in range(shares):
        own = slice(t * own_columns, (t + 1) * own_columns)
        share_out[t] = jnp.concatenate(
            [sums[:, b * short : (b + 1) * short, own] for b in range(fold)], axis=2
        ).astype(share_out.dtype)
    shared = []
    for off in range(1, shares):
        target = lax.rem(me_sub + off, shares)
        shared.append(send(share_out.at[target], share_in.at[off - 1], 0, off))
        shared.append(send(mass_row.at[0], mass_row.at[off], 0, off))
    everything += shared
    for copy in shared:
        copy.wait_recv()
    share = share_out[me_sub].astype(F32)
    for off in range(1, shares):
        share = share + share_in[off - 1].astype(F32)
    back_out[...] = share
    mass_all = mass_row[0]
    for off in range(1, shares):
        mass_all = mass_all + mass_row[off]
    stats = jnp.where(iota((8, total), 0) == 0, mass_all, peak)
    for g in range(groups):
        mine = stats[:, g * CAP : (g + 1) * CAP]
        stat_out[g] = jnp.concatenate([mine, jnp.zeros((8, LANES - CAP), F32)], axis=1)
    returned = []
    for off in range(1, groups):
        target = lax.rem(me_cell + off, groups)
        returned.append(send(back_out.at[target], back_in.at[me_cell], off, 0))
        returned.append(send(stat_out.at[target], stat_in.at[me_cell], off, 0))
    everything += returned
    back_in[me_cell] = back_out[me_cell]
    stat_in[me_cell] = stat_out[me_cell]

    first, second, _, earlier = positions(meta_ref, groups)
    marks = []
    for route, named in ((0, first), (1, second)):
        spot = jnp.sum(
            named * earlier, axis=0, keepdims=True
        ).astype(jnp.int32)
        slot = meta_ref[route : route + 1, :] * CAP + spot
        marks.append((iota((total, count), 0) == slot).astype(F32).astype(BF16))
    for copy in returned:
        copy.wait_recv()

    def pick(array, mark, dim):
        out = 0.0
        for _ in range(3):
            piece = array.astype(BF16)
            out = out + lax.dot_general(
                piece, mark, (((dim,), (0,)), ((), ())), preferred_element_type=F32
            )
            array = array - piece.astype(F32)
        return out

    held = back_in[...]
    table = jnp.concatenate(
        [held[:, :, b * own_columns : (b + 1) * own_columns] for b in range(fold)], axis=1
    ).reshape(total, own_columns)
    stat_row = jnp.concatenate([stat_in[g][:, :CAP] for g in range(groups)], axis=1)
    stat_0, stat_1 = pick(stat_row, marks[0], 1), pick(stat_row, marks[1], 1)
    top = jnp.maximum(stat_0[1:2], stat_1[1:2])
    scale_0, scale_1 = jnp.exp(stat_0[1:2] - top), jnp.exp(stat_1[1:2] - top)
    lower = scale_0 * stat_0[0:1] + scale_1 * stat_1[0:1]
    upper = scale_0 * pick(table, marks[0], 0) + scale_1 * pick(table, marks[1], 0)
    columns[me_sub] = (upper / lower).astype(BF16)
    gathered = [
        send(columns.at[me_sub], columns.at[me_sub], 0, off) for off in range(1, shares)
    ]
    everything += gathered
    for copy in gathered:
        copy.wait_recv()
    pooled_ref[...] = jnp.transpose(
        columns[...].astype(F32).reshape(width, count)
    ).astype(BF16)
    for copy in everything:
        copy.wait_send()


def local(queries, probe_groups, probe_cells, coarse, codebooks, codes, lengths, payload):
    groups, shares = lax.axis_size("cell"), lax.axis_size("sub")
    count, own_width = queries.shape
    half = probe_cells.shape[2]
    cells, own_subs, row_slots = codes.shape
    row_local = row_slots // shares
    rows = cells * row_local
    total = groups * CAP
    width = payload.shape[2]
    fold = LANES // (width // shares)
    short = CAP // fold
    meta = jnp.concatenate([probe_groups, probe_cells.reshape(count, -1)], axis=1).T
    sent_codes = jnp.transpose(
        codes.astype(BF16).reshape(cells, own_subs, shares, row_local), (2, 1, 0, 3)
    ).reshape(shares, own_subs, rows)
    copies = 3 * (shares - 1) + 4 * (groups - 1) + (groups + 4) * (shares - 1)
    spec = pl.BlockSpec(memory_space=pltpu.VMEM)
    return pl.pallas_call(
        functools.partial(whole_kernel, groups, shares, half, row_local, fold),
        out_shape=jax.ShapeDtypeStruct((count, width), BF16),
        in_specs=[spec] * 7,
        out_specs=spec,
        scratch_shapes=[
            pltpu.VMEM((groups, CAP, own_width), BF16),
            pltpu.VMEM((groups, CAP, LANES), BF16),
            pltpu.VMEM((shares, groups, CAP, own_width), BF16),
            pltpu.VMEM((groups, CAP, LANES), BF16),
            pltpu.VMEM((shares - 1, own_subs, rows), BF16),
            pltpu.VMEM((shares - 1,) + codebooks.shape, BF16),
            pltpu.VMEM((shares - 1,) + coarse.shape, BF16),
            pltpu.VMEM((own_subs, rows), jnp.int32),
            pltpu.VMEM((shares * own_width, rows), BF16),
            pltpu.VMEM((8, rows), F32),
            pltpu.VMEM((total, LANES), F32),
            pltpu.VMEM((total, rows), F32),
            pltpu.VMEM((shares, 8, total), F32),
            pltpu.VMEM((total, width), F32),
            pltpu.VMEM((total, LANES), F32),
            pltpu.VMEM((shares, 8, total), F32),
            pltpu.VMEM((shares, groups, short, LANES), F32),
            pltpu.VMEM((shares - 1, groups, short, LANES), F32),
            pltpu.VMEM((groups, short, LANES), F32),
            pltpu.VMEM((groups, short, LANES), F32),
            pltpu.VMEM((groups, 8, LANES), F32),
            pltpu.VMEM((groups, 8, LANES), F32),
            pltpu.VMEM((shares, width // shares, count), BF16),
            pltpu.SemaphoreType.DMA((copies,)),
            pltpu.SemaphoreType.DMA((copies,)),
        ],
        compiler_params=pltpu.CompilerParams(
            collective_id=0, has_side_effects=True, vmem_limit_bytes=56 * 1024 * 1024
        ),
    )(meta, queries, sent_codes, codebooks, coarse, lengths.reshape(cells, 1), payload.reshape(rows, width))


def solution(mesh):
    placed = (
        P("cell", "sub"),
        P("cell", None),
        P("cell", None, None),
        P("cell", "sub"),
        P("sub", None, None),
        P("cell", "sub", None),
        P("cell"),
        P("cell", "sub", None),
    )
    return jax.shard_map(
        local, mesh=mesh, in_specs=placed, out_specs=P("cell", None), check_vma=False
    )
```

time: 166 us -> 73.8 us (0.44)
  blocking collectives: 80.3 us -> 0 us
  Pallas kernels: 29.2 us -> 67.2 us
  waiting for transfers between devices: 27.8 us -> 0 us
  between operations: 13.5 us -> 0.05 us
  starting transfers between devices: 7.11 us -> 0 us
    pallas_call x4 -> x1, Pallas kernels: 29.2 us -> 67.2 us  [local(): pl.pallas_call(functools.partial(whole_kernel, groups, shares, half, row_...]
    all_gather x3 -> x0, blocking collectives: 31.9 us -> none  [the longest x1 12.1 us: local(): back = lax.all_gather(back, 'sub', axis=1, tiled=True).reshape(total, wide)]
    all_to_all x2 -> x0, blocking collectives: 28.9 us -> none  [the longest x1 16 us: swap(): lax.all_to_all(array.reshape(groups, shape[0] // groups, shape[1]), 'cell...]
    reduce_scatter x1 -> x0, waiting for transfers between devices: 24.4 us -> none  [local(): lax.psum_scatter(sums.reshape(groups, CAP, wide), 'sub', scatter_dimensio...]
    pmax x1 -> x0, blocking collectives: 19.5 us -> none  [local(): peak = lax.pmax(peak, 'sub')]
    all_to_all x2 -> x0, starting transfers between devices: 7.1 us -> none  [the longest x1 3.72 us: local(): lax.all_to_all(sent_codes, 'sub', split_axis=0, concat_axis=0, tiled=True)]
    all_to_all x2 -> x0, waiting for transfers between devices: 3.32 us -> none  [the longest x1 3.31 us: swap(): lax.all_to_all(array.reshape(groups, shape[0] // groups, shape[1]), 'cell...]
  transfers between devices with their start and end apart: 4 -> 0, of which waited for: 2 -> 0; matrix products, arithmetic and copies ran while one was open for 2% -> 0% of each run, Pallas kernels for 0% -> 0%
where the time goes in v2:
time: 73.8 us; the launch traced here: 73.5 us
  Pallas kernels  67.2 us (91%)
  local copies, waits for them, and re-layouts  4.45 us (6%)
  other arithmetic  1.81 us (2%)
    pallas_call x1, Pallas kernels, local(): pl.pallas_call(functools.partial(whole_kernel, groups, shares, half, row_...  67.2 us
    unnamed x7, local copies, waits for them, and re-layouts  1.59 us
    reshape x1, local copies, waits for them, and re-layouts, local(): sent_codes = jnp.transpose(codes.astype(BF16).reshape(cells, own_subs, sh...  1.48 us

profile of v2, /device:TPU:0, one launch (start us, length us, event | category | flops | bytes accessed | tf_op | source)
XLA Modules:
  0.0 73.5 jit_solution(9327960468551965649)
XLA Ops:
  0.0 1.2 %convert_element_type.3 = bf16[32,16,384]{2,1,0:T(8,128)(2,1)S(1)} convert(s32[32,16,384]{2,1,0:T(8,128)} %param.13) | non-fusion elementwise | flops 196608 | bytes 1179648 | tf_op jit(solution)/shard_map/convert_element_type | solution.py:405
  1.2 0.0 copy-start
  1.2 0.0 copy-start.1
  1.2 0.0 copy-start.2
  1.2 0.4 reshape.16
  1.6 0.3 copy.12
  1.9 1.5 %reshape.17.codes_ref = bf16[4,16,3072]{2,1,0:T(8,128)(2,1)} reshape(bf16[4,16,32,96]{3,2,1,0:T(8,128)(2,1)S(1)} %bitcast.10) | data formatting | bytes 786432 | tf_op jit(solution)/shard_map/reshape | solution.py:406
  3.4 0.0 copy-done
  3.4 0.0 copy-done.1
  3.4 0.6 add_bitcast_fusion.meta_ref
  4.0 0.0 copy-done.2
  4.1 0.7 copy.10.lengths_ref
  4.7 67.2 %shard_map.82 = bf16[256,256]{1,0:T(8,128)(2,1)} custom-call(s32[34,256]{1,0:T(8,128)} %add_bitcast_fusion.meta_ref, bf16[256,256]{1,0:T(8,128)(2,1)} %rows_ref.1, bf16[4,16,3072]{2,1,0:T(8,128)(2,1)} %reshape.17.codes_ref, bf16[16,16,256]{2,1,0:T(8,128)(2,1)} %books_ref.1, bf16[32,256]{1,0:T(8,128)(2,1)} %coarse_ref.1, s32[32,1]{1,0:T(8,128)} %copy.10.lengths_ref, ...), custom_call_target="tpu_custom_call" | custom-call | tf_op jit(solution)/shard_map/pallas_call | solution.py:409
  72.0 1.6 %copy.14 = bf16[256,256]{1,0:T(8,128)(2,1)} copy(bf16[256,256]{1,0:T(8,128)(2,1)} %shard_map.82) | data formatting | bytes 262144
Async XLA Ops:
  1.2 2.2 %copy-start = (s32[256,2,16]{0,2,1:T(8,128)S(1)}, s32[256,2,16]{0,2,1:T(8,128)}, u32[]{:S(2)}) copy-start(s32[256,2,16]{0,2,1:T(8,128)} %param.10) | copy-start | bytes 98308
  1.2 2.2 %copy-start.1 = (s32[256,2]{0,1:T(2,128)S(1)}, s32[256,2]{0,1:T(2,128)}, u32[]{:S(2)}) copy-start(s32[256,2]{0,1:T(2,128)} %param.9) | copy-start | bytes 6148
  1.2 2.8 %copy-start.2 = (s32[32]{0:T(128)S(1)}, s32[32]{0:T(128)}, u32[]{:S(2)}) copy-start(s32[32]{0:T(128)} %param.14) | copy-start | bytes 388

commit v3 on v2

--- a/solution.py
+++ b/solution.py
@@ -1,4 +1,5 @@
 import functools
+import math
 
 import jax
 import jax.numpy as jnp
@@ -8,6 +9,7 @@
 from jax.sharding import PartitionSpec as P
 
 CAP = 64
+HALVES = 2
 LANES = 128
 score_scale = 0.3
 floor_score = -1e30
@@ -102,12 +104,13 @@
     fold,
     meta_ref,
     rows_ref,
-    codes_ref,
+    raw_codes_ref,
     books_ref,
     coarse_ref,
     lengths_ref,
     payload_ref,
     pooled_ref,
+    codes_ref,
     buffer,
     away_out,
     queries,
@@ -142,7 +145,7 @@
     total = groups * CAP
     width = payload_ref.shape[1]
     own_columns = width // shares
-    short = CAP // fold
+    short = CAP // fold // HALVES
     blocks = rows // LANES
     step = 512 if rows % 512 == 0 else 256
     used = [0]
@@ -173,9 +176,30 @@
         pl.semaphore_signal(
             barrier, inc=1, device_id=device(0, off), device_id_type=pl.DeviceIdType.MESH
         )
+    several = LANES // math.gcd(row_local, LANES)
+    for t in range(shares):
+        for start in range(0, cells, several):
+            codes_ref[t, :, start * row_local : (start + several) * row_local] = jnp.concatenate(
+                [
+                    raw_codes_ref[c, :, t * row_local : (t + 1) * row_local]
+                    for c in range(start, start + several)
+                ],
+                axis=1,
+            ).astype(F32).astype(BF16)
+    pack_kernel(groups, half, meta_ref, rows_ref, buffer, away_out)
     pl.semaphore_wait(barrier, groups + shares - 2)
 
     everything = []
+    routed = [None]
+    for off in range(1, groups):
+        target = lax.rem(me_cell + off, groups)
+        routed.append(
+            [
+                send(buffer.at[target], queries.at[0, me_cell], off, 0),
+                send(away_out.at[target], away.at[me_cell], off, 0),
+            ]
+        )
+        everything += routed[-1]
     lists = [None]
     for off in range(1, shares):
         target = lax.rem(me_sub + off, shares)
@@ -188,17 +212,6 @@
         )
         everything += lists[-1]
 
-    pack_kernel(groups, half, meta_ref, rows_ref, buffer, away_out)
-    routed = [None]
-    for off in range(1, groups):
-        target = lax.rem(me_cell + off, groups)
-        routed.append(
-            [
-                send(buffer.at[target], queries.at[0, me_cell], off, 0),
-                send(away_out.at[target], away.at[me_cell], off, 0),
-            ]
-        )
-        everything += routed[-1]
     queries[0, me_cell] = buffer[me_cell]
     away[me_cell] = away_out[me_cell]
     spread_out = []
@@ -250,98 +263,127 @@
 
     offset = iota((cells, rows), 1) - iota((cells, rows), 0) * row_local
     inside = (offset >= 0) & (offset < row_local)
+    reach = jnp.zeros((cells, 1), jnp.int32)
+    for c in range(cells):
+        reach = jnp.where(iota((cells, 1), 0) == c, lengths_ref[c], reach)
     live = jnp.sum(
-        (inside & (offset + me_sub * row_local < lengths_ref[...])).astype(F32),
+        (inside & (offset + me_sub * row_local < reach)).astype(F32),
         axis=0,
         keepdims=True,
     )
     half_norm = 0.5 * jnp.sum(squares[...], axis=0, keepdims=True)
     squares[0:1, :] = jnp.where(live > 0.5, half_norm, -floor_score)
-    best[...] = jnp.full_like(best, 3.0 * floor_score)
     for copy in spread_out:
         copy.wait_recv()
-
-    @pl.loop(0, rows // step)
-    def _(n):
-        lanes = pl.ds(pl.multiple_of(n * step, step), step)
-        shift = iota((LANES, step), 1) + n * step - iota((LANES, step), 0) * row_local
-        far = jnp.where((shift >= 0) & (shift < row_local), floor_score, 0.0).astype(BF16)
-        raw = jnp.dot(away[...].reshape(total, LANES), far, preferred_element_type=F32)
-        for k in range(shares):
-            raw = raw + jnp.dot(
-                queries[k].reshape(total, own_width),
-                vectors[k * own_width : (k + 1) * own_width, lanes],
+    part_cap = CAP // HALVES
+    part_total = total // HALVES
+
+    def score(h):
+        some = slice(h * part_cap, (h + 1) * part_cap)
+        best[h] = jnp.full(best.shape[1:], 3.0 * floor_score, F32)
+
+        @pl.loop(0, rows // step)
+        def _(n):
+            lanes = pl.ds(pl.multiple_of(n * step, step), step)
+            shift = iota((LANES, step), 1) + n * step - iota((LANES, step), 0) * row_local
+            far = jnp.where((shift >= 0) & (shift < row_local), floor_score, 0.0).astype(BF16)
+            raw = jnp.dot(
+                away[:, some].reshape(part_total, LANES), far, preferred_element_type=F32
+            )
+            for k in range(shares):
+                raw = raw + jnp.dot(
+                    queries[k, :, some].reshape(part_total, own_width),
+                    vectors[k * own_width : (k + 1) * own_width, lanes],
+                    preferred_element_type=F32,
+                )
+            scores = (raw - squares[0:1, lanes]) * score_scale
+            values[h, :, lanes] = scores
+            top = best[h]
+            for b in range(step // LANES):
+                top = jnp.maximum(top, scores[:, b * LANES : (b + 1) * LANES])
+            best[h] = top
+
+        peak_row[h, 0] = jnp.broadcast_to(
+            jnp.max(jnp.transpose(best[h]), axis=0, keepdims=True), (8, part_total)
+        )
+        return [
+            send(peak_row.at[h, 0], peak_row.at[h, off], 0, off) for off in range(1, shares)
+        ]
+
+    def pool(h, tops):
+        for copy in tops:
+            copy.wait_recv()
+        peak = jnp.max(peak_row[h], axis=0)
+        best[h] = jnp.transpose(jnp.broadcast_to(peak[0:1], (LANES, part_total)))
+        part[...] = jnp.zeros_like(part)
+        masses[...] = jnp.zeros_like(masses)
+
+        @pl.loop(0, rows // step)
+        def _(n):
+            lanes = pl.ds(pl.multiple_of(n * step, step), step)
+            mass = masses[...]
+            pieces = []
+            for b in range(step // LANES):
+                inner = pl.ds(pl.multiple_of(n * step + b * LANES, LANES), LANES)
+                piece = jnp.exp(values[h, :, inner] - best[h]).astype(BF16)
+                mass = mass + piece.astype(F32)
+                pieces.append(piece)
+            masses[...] = mass
+            part[...] += jnp.dot(
+                jnp.concatenate(pieces, axis=1),
+                payload_ref[lanes, :],
                 preferred_element_type=F32,
             )
-        scores = (raw - squares[0:1, lanes]) * score_scale
-        values[:, lanes] = scores
-        top = best[...]
-        for b in range(step // LANES):
-            top = jnp.maximum(top, scores[:, b * LANES : (b + 1) * LANES])
-        best[...] = top
-
-    peak_row[0] = jnp.broadcast_to(
-        jnp.max(jnp.transpose(best[...]), axis=0, keepdims=True), (8, total)
-    )
-    tops = [send(peak_row.at[0], peak_row.at[off], 0, off) for off in range(1, shares)]
-    everything += tops
-    for copy in tops:
-        copy.wait_recv()
-    peak = jnp.max(peak_row[...], axis=0)
-    best[...] = jnp.transpose(jnp.broadcast_to(peak[0:1], (LANES, total)))
-    part[...] = jnp.zeros_like(part)
-    masses[...] = jnp.zeros_like(masses)
-
-    @pl.loop(0, rows // step)
-    def _(n):
-        lanes = pl.ds(pl.multiple_of(n * step, step), step)
-        mass = masses[...]
-        pieces = []
-        for b in range(step // LANES):
-            inner = pl.ds(pl.multiple_of(n * step + b * LANES, LANES), LANES)
-            piece = jnp.exp(values[:, inner] - best[...]).astype(BF16)
-            mass = mass + piece.astype(F32)
-            pieces.append(piece)
-        masses[...] = mass
-        part[...] += jnp.dot(
-            jnp.concatenate(pieces, axis=1), payload_ref[lanes, :], preferred_element_type=F32
-        )
-
-    mass_row[0] = jnp.broadcast_to(
-        jnp.sum(jnp.transpose(masses[...]), axis=0, keepdims=True), (8, total)
-    )
-    sums = part[...].reshape(groups, CAP, width)
-    for t in range(shares):
-        own = slice(t * own_columns, (t + 1) * own_columns)
-        share_out[t] = jnp.concatenate(
-            [sums[:, b * short : (b + 1) * short, own] for b in range(fold)], axis=2
-        ).astype(share_out.dtype)
-    shared = []
-    for off in range(1, shares):
-        target = lax.rem(me_sub + off, shares)
-        shared.append(send(share_out.at[target], share_in.at[off - 1], 0, off))
-        shared.append(send(mass_row.at[0], mass_row.at[off], 0, off))
-    everything += shared
-    for copy in shared:
-        copy.wait_recv()
-    share = share_out[me_sub].astype(F32)
-    for off in range(1, shares):
-        share = share + share_in[off - 1].astype(F32)
-    back_out[...] = share
-    mass_all = mass_row[0]
-    for off in range(1, shares):
-        mass_all = mass_all + mass_row[off]
-    stats = jnp.where(iota((8, total), 0) == 0, mass_all, peak)
+
+        mass_row[h, 0] = jnp.broadcast_to(
+            jnp.sum(jnp.transpose(masses[...]), axis=0, keepdims=True), (8, part_total)
+        )
+        sums = part[...].reshape(groups, part_cap, width)
+        for t in range(shares):
+            own = slice(t * own_columns, (t + 1) * own_columns)
+            share_out[h, t] = jnp.concatenate(
+                [sums[:, b * short : (b + 1) * short, own] for b in range(fold)], axis=2
+            ).astype(share_out.dtype)
+        shared = []
+        for off in range(1, shares):
+            target = lax.rem(me_sub + off, shares)
+            shared.append(send(share_out.at[h, target], share_in.at[h, off - 1], 0, off))
+            shared.append(send(mass_row.at[h, 0], mass_row.at[h, off], 0, off))
+        return shared, peak
+
+    def give_back(h, shared, peak):
+        for copy in shared:
+            copy.wait_recv()
+        share = share_out[h, me_sub].astype(F32)
+        for off in range(1, shares):
+            share = share + share_in[h, off - 1].astype(F32)
+        back_out[h] = share
+        sent = []
+        for off in range(1, groups):
+            target = lax.rem(me_cell + off, groups)
+            sent.append(send(back_out.at[h, target], back_in.at[h, me_cell], off, 0))
+        back_in[h, me_cell] = back_out[h, me_cell]
+        mass_all = mass_row[h, 0]
+        for off in range(1, shares):
+            mass_all = mass_all + mass_row[h, off]
+        return sent, jnp.where(iota((8, part_total), 0) == 0, mass_all, peak)
+
+    tops = [score(h) for h in range(HALVES)]
+    pooled = [pool(h, tops[h]) for h in range(HALVES)]
+    given = [give_back(h, *pooled[h]) for h in range(HALVES)]
+    returned = []
+    for h in range(HALVES):
+        everything += tops[h] + pooled[h][0] + given[h][0]
+        returned += given[h][0]
     for g in range(groups):
-        mine = stats[:, g * CAP : (g + 1) * CAP]
-        stat_out[g] = jnp.concatenate([mine, jnp.zeros((8, LANES - CAP), F32)], axis=1)
-    returned = []
+        mine = [stats[:, g * part_cap : (g + 1) * part_cap] for _, stats in given]
+        stat_out[g] = jnp.concatenate(mine + [jnp.zeros((8, LANES - CAP), F32)], axis=1)
+    stat_sent = []
     for off in range(1, groups):
         target = lax.rem(me_cell + off, groups)
-        returned.append(send(back_out.at[target], back_in.at[me_cell], off, 0))
-        returned.append(send(stat_out.at[target], stat_in.at[me_cell], off, 0))
-    everything += returned
-    back_in[me_cell] = back_out[me_cell]
+        stat_sent.append(send(stat_out.at[target], stat_in.at[me_cell], off, 0))
+    everything += stat_sent
+    returned += stat_sent
     stat_in[me_cell] = stat_out[me_cell]
 
     first, second, _, earlier = positions(meta_ref, groups)
@@ -365,9 +407,13 @@
             array = array - piece.astype(F32)
         return out
 
-    held = back_in[...]
     table = jnp.concatenate(
-        [held[:, :, b * own_columns : (b + 1) * own_columns] for b in range(fold)], axis=1
+        [
+            back_in[h][:, :, b * own_columns : (b + 1) * own_columns]
+            for h in range(HALVES)
+            for b in range(fold)
+        ],
+        axis=1,
     ).reshape(total, own_columns)
     stat_row = jnp.concatenate([stat_in[g][:, :CAP] for g in range(groups)], axis=1)
     stat_0, stat_1 = pick(stat_row, marks[0], 1), pick(stat_row, marks[1], 1)
@@ -382,9 +428,7 @@
     everything += gathered
     for copy in gathered:
         copy.wait_recv()
-    pooled_ref[...] = jnp.transpose(
-        columns[...].astype(F32).reshape(width, count)
-    ).astype(BF16)
+    pooled_ref[...] = columns[...].reshape(width, count)
     for copy in everything:
         copy.wait_send()
 
@@ -399,19 +443,17 @@
     total = groups * CAP
     width = payload.shape[2]
     fold = LANES // (width // shares)
-    short = CAP // fold
+    short = CAP // fold // HALVES
     meta = jnp.concatenate([probe_groups, probe_cells.reshape(count, -1)], axis=1).T
-    sent_codes = jnp.transpose(
-        codes.astype(BF16).reshape(cells, own_subs, shares, row_local), (2, 1, 0, 3)
-    ).reshape(shares, own_subs, rows)
-    copies = 3 * (shares - 1) + 4 * (groups - 1) + (groups + 4) * (shares - 1)
+    copies = (3 + HALVES) * (groups - 1) + (groups + 4 + 3 * HALVES) * (shares - 1)
     spec = pl.BlockSpec(memory_space=pltpu.VMEM)
-    return pl.pallas_call(
+    pooled = pl.pallas_call(
         functools.partial(whole_kernel, groups, shares, half, row_local, fold),
-        out_shape=jax.ShapeDtypeStruct((count, width), BF16),
-        in_specs=[spec] * 7,
+        out_shape=jax.ShapeDtypeStruct((width, count), BF16),
+        in_specs=[spec] * 5 + [pl.BlockSpec(memory_space=pltpu.SMEM), spec],
         out_specs=spec,
         scratch_shapes=[
+            pltpu.VMEM((shares, own_subs, rows), BF16),
             pltpu.VMEM((groups, CAP, own_width), BF16),
             pltpu.VMEM((groups, CAP, LANES), BF16),
             pltpu.VMEM((shares, groups, CAP, own_width), BF16),
@@ -422,16 +464,16 @@
             pltpu.VMEM((own_subs, rows), jnp.int32),
             pltpu.VMEM((shares * own_width, rows), BF16),
             pltpu.VMEM((8, rows), F32),
-            pltpu.VMEM((total, LANES), F32),
-            pltpu.VMEM((total, rows), F32),
-            pltpu.VMEM((shares, 8, total), F32),
-            pltpu.VMEM((total, width), F32),
-            pltpu.VMEM((total, LANES), F32),
-            pltpu.VMEM((shares, 8, total), F32),
-            pltpu.VMEM((shares, groups, short, LANES), F32),
-            pltpu.VMEM((shares - 1, groups, short, LANES), F32),
-            pltpu.VMEM((groups, short, LANES), F32),
-            pltpu.VMEM((groups, short, LANES), F32),
+            pltpu.VMEM((HALVES, total // HALVES, LANES), F32),
+            pltpu.VMEM((HALVES, total // HALVES, rows), F32),
+            pltpu.VMEM((HALVES, shares, 8, total // HALVES), F32),
+            pltpu.VMEM((total // HALVES, width), F32),
+            pltpu.VMEM((total // HALVES, LANES), F32),
+            pltpu.VMEM((HALVES, shares, 8, total // HALVES), F32),
+            pltpu.VMEM((HALVES, shares, groups, short, LANES), BF16),
+            pltpu.VMEM((HALVES, shares - 1, groups, short, LANES), BF16),
+            pltpu.VMEM((HALVES, groups, short, LANES), F32),
+            pltpu.VMEM((HALVES, groups, short, LANES), F32),
             pltpu.VMEM((groups, 8, LANES), F32),
             pltpu.VMEM((groups, 8, LANES), F32),
             pltpu.VMEM((shares, width // shares, count), BF16),
@@ -441,7 +483,8 @@
         compiler_params=pltpu.CompilerParams(
             collective_id=0, has_side_effects=True, vmem_limit_bytes=56 * 1024 * 1024
         ),
-    )(meta, queries, sent_codes, codebooks, coarse, lengths.reshape(cells, 1), payload.reshape(rows, width))
+    )(meta, queries, codes, codebooks, coarse, lengths, payload.reshape(rows, width))
+    return pooled.T
 
 
 def solution(mesh):

time: 73.8 us -> 66.4 us (0.90)
  Pallas kernels: 67.2 us -> 63.1 us
  local copies, waits for them, and re-layouts: 4.45 us -> 1.66 us
    pallas_call x1, Pallas kernels: 67.2 us -> 63.1 us  [local(): pl.pallas_call(functools.partial(whole_kernel, groups, shares, half, row_...]
    reshape x4 -> x0, local copies, waits for them, and re-layouts: 2.87 us -> none  [the longest x1 1.48 us: local(): sent_codes = jnp.transpose(codes.astype(BF16).reshape(cells, own_subs, sh...]
    transpose x0 -> x1, local copies, waits for them, and re-layouts: none -> 1.66 us  [local(): return pooled.T]
    unnamed x7 -> x0, local copies, waits for them, and re-layouts: 1.59 us -> none
    convert_element_type x1 -> x0, other arithmetic: 1.18 us -> none  [local(): codes.astype(BF16).reshape(cells, own_subs, shares, row_local)]
    transpose x1, other arithmetic: 0.62 us -> 1.38 us  [local(): jnp.concatenate([probe_groups, probe_cells.reshape(count, -1)], axis=1)]
where the time goes in v3:
time: 66.4 us; the launch traced here: 66.1 us
  Pallas kernels  63.1 us (95%)
  local copies, waits for them, and re-layouts  1.66 us (2%)
  other arithmetic  1.38 us (2%)
    pallas_call x1, Pallas kernels, local(): pl.pallas_call(functools.partial(whole_kernel, groups, shares, half, row_...  63.1 us
    transpose x1, local copies, waits for them, and re-layouts, local(): return pooled.T  1.66 us
    transpose x1, other arithmetic, local(): jnp.concatenate([probe_groups, probe_cells.reshape(count, -1)], axis=1)  1.38 us

profile of v3, /device:TPU:0, one launch (start us, length us, event | category | flops | bytes accessed | tf_op | source)
XLA Modules:
  0.0 66.1 jit_solution(9302931745439455589)
XLA Ops:
  0.0 1.4 %add_bitcast_fusion.meta_ref = s32[34,256]{1,0:T(8,128)} fusion(s32[256,32]{0,1:T(8,128)} %bitcast.7, s32[256,2]{0,1:T(2,128)} %param.9), kind=kLoop, calls=%fused_computation | loop fusion | flops 8704 | bytes 69632 | tf_op jit(solution)/shard_map/transpose | solution.py:447
  1.4 63.1 %shard_map.82 = bf16[256,256]{1,0:T(8,128)(2,1)} custom-call(s32[34,256]{1,0:T(8,128)} %add_bitcast_fusion.meta_ref, bf16[256,256]{1,0:T(8,128)(2,1)} %rows_ref.1, s32[32,16,384]{2,1,0:T(8,128)} %raw_codes_ref.1, bf16[16,16,256]{2,1,0:T(8,128)(2,1)} %books_ref.1, bf16[32,256]{1,0:T(8,128)(2,1)} %coarse_ref.1, s32[32]{0:T(128)} %lengths_ref.1, ...), custom_call_target="tpu_custom_call" | custom-call | tf_op jit(solution)/shard_map/pallas_call | solution.py:450
  64.5 1.7 %copy.9 = bf16[256,256]{1,0:T(8,128)(2,1)} copy(bf16[256,256]{0,1:T(8,128)(2,1)} %bitcast.6) | data formatting | bytes 262144 | tf_op jit(solution)/shard_map/transpose | solution.py:487

commit v4 on v3

--- a/solution.py
+++ b/solution.py
@@ -59,41 +59,37 @@
         away_ref[g] = (1.0 - there).astype(BF16)
 
 
-def decode_share(subs, width, blocks, codes_ref, books_ref, base, ids, vectors, squares):
+def decode_share(subs, width, blocks, codes_ref, books_ref, base, ids, tables, centers, vectors, squares):
     near = min(8, subs)
     ids[...] = codes_ref[...].astype(F32).astype(jnp.int32)
-
-    def some(start):
+    tables[...] = books_ref[...].astype(F32)
+    for start in range(0, subs, near):
+
         @pl.loop(0, blocks // 2)
         def _(pair):
             for u in range(2):
                 lanes = pl.ds(pl.multiple_of(pair * (2 * LANES) + u * LANES, LANES), LANES)
-                held = ids[pl.ds(start, near), lanes]
-                total = jnp.zeros((8, LANES), F32)
-                for j in range(near):
-                    book = books_ref[start + j].astype(F32)
-                    code = jnp.broadcast_to(held[j : j + 1, :], (width, LANES))
+                inner = slice(start * width, (start + near) * width)
+                around = centers[inner, lanes].astype(F32)
+                found = []
+                for j in range(start, start + near):
+                    code = jnp.broadcast_to(ids[j : j + 1, lanes], (8, LANES))
                     index = code & (LANES - 1)
-                    picked = jnp.where(
-                        code < LANES,
-                        jnp.take_along_axis(book[:, :LANES], index, axis=1, mode="promise_in_bounds"),
-                        jnp.take_along_axis(book[:, LANES:], index, axis=1, mode="promise_in_bounds"),
-                    )
-                    place = pl.ds(pl.multiple_of(base + (start + j) * width, width), width)
-                    summed = (picked + vectors[place, lanes].astype(F32)).astype(BF16)
-                    vectors[place, lanes] = summed
-                    back = summed.astype(F32)
-                    back = back * back
-                    total += back[:8] + back[8:]
-                squares[:, lanes] += total
-
-    if subs == near:
-        some(0)
-    else:
-
-        @pl.loop(0, subs // near)
-        def _(group):
-            some(pl.multiple_of(group * near, near))
+                    for d in range(0, width, 8):
+                        low = tables[j, d : d + 8, :LANES]
+                        high = tables[j, d : d + 8, LANES:]
+                        found.append(
+                            jnp.where(
+                                code < LANES,
+                                jnp.take_along_axis(low, index, axis=1, mode="promise_in_bounds"),
+                                jnp.take_along_axis(high, index, axis=1, mode="promise_in_bounds"),
+                            )
+                        )
+                summed = (jnp.concatenate(found, axis=0) + around).astype(BF16)
+                vectors[base + start * width : base + (start + near) * width, lanes] = summed
+                back = summed.astype(F32)
+                back = back * back
+                squares[:, lanes] += jnp.sum(back.reshape(-1, 8, LANES), axis=0)
 
 
 def whole_kernel(
@@ -119,6 +115,8 @@
     books_in,
     coarse_in,
     ids,
+    tables,
+    spread,
     vectors,
     squares,
     best,
@@ -153,7 +151,7 @@
     def device(cell_off, sub_off):
         return (lax.rem(me_cell + cell_off, groups), lax.rem(me_sub + sub_off, shares))
 
-    def send(src, dst, cell_off, sub_off):
+    def send(src, dst, cell_off, sub_off, target=None):
         i = used[0]
         used[0] += 1
         copy = pltpu.make_async_remote_copy(
@@ -161,7 +159,7 @@
             dst_ref=dst,
             send_sem=send_sem.at[i],
             recv_sem=recv_sem.at[i],
-            device_id=device(cell_off, sub_off),
+            device_id=target or device(cell_off, sub_off),
             device_id_type=pl.DeviceIdType.MESH,
         )
         copy.start()
@@ -200,16 +198,21 @@
             ]
         )
         everything += routed[-1]
-    lists = [None]
+    core = lax.rem(me_cell, 2)
+    beside = (me_cell + 1 - 2 * core, me_sub)
+    split = subs // 2
+    mine = pl.ds(core * split, split)
+    lists, halves = [None], [None]
     for off in range(1, shares):
         target = lax.rem(me_sub + off, shares)
         lists.append(
             [
                 send(codes_ref.at[target], codes_in.at[off - 1], 0, off),
-                send(books_ref, books_in.at[off - 1], 0, off),
                 send(coarse_ref, coarse_in.at[off - 1], 0, off),
             ]
         )
+        halves.append(send(books_ref.at[mine], books_in.at[off - 1, mine], 0, off))
+        everything.append(halves[-1])
         everything += lists[-1]
 
     queries[0, me_cell] = buffer[me_cell]
@@ -230,6 +233,12 @@
     squares[...] = jnp.zeros_like(squares)
     passed = 1
     for k in range(shares):
+        if k == 1:
+            for off in range(1, shares):
+                halves[off].wait_recv()
+                here = books_in.at[off - 1, mine]
+                lists[off].append(send(here, here, 0, 0, beside))
+                everything.append(lists[off][-1])
         if k:
             for copy in lists[k]:
                 copy.wait_recv()
@@ -240,7 +249,7 @@
             lanes = pl.ds(pl.multiple_of(n * step, step), step)
             shift = iota((cells, step), 1) + n * step - iota((cells, step), 0) * row_local
             inside = ((shift >= 0) & (shift < row_local)).astype(F32).astype(BF16)
-            vectors[k * own_width : (k + 1) * own_width, lanes] = lax.dot_general(
+            spread[:, lanes] = lax.dot_general(
                 centers[...], inside, (((0,), (0,)), ((), ())), preferred_element_type=F32
             ).astype(BF16)
 
@@ -252,6 +261,8 @@
             books_in.at[k - 1] if k else books_ref,
             k * own_width,
             ids,
+            tables,
+            spread,
             vectors,
             squares,
         )
@@ -445,7 +456,7 @@
     fold = LANES // (width // shares)
     short = CAP // fold // HALVES
     meta = jnp.concatenate([probe_groups, probe_cells.reshape(count, -1)], axis=1).T
-    copies = (3 + HALVES) * (groups - 1) + (groups + 4 + 3 * HALVES) * (shares - 1)
+    copies = (3 + HALVES) * (groups - 1) + (groups + 5 + 3 * HALVES) * (shares - 1)
     spec = pl.BlockSpec(memory_space=pltpu.VMEM)
     pooled = pl.pallas_call(
         functools.partial(whole_kernel, groups, shares, half, row_local, fold),
@@ -462,6 +473,8 @@
             pltpu.VMEM((shares - 1,) + codebooks.shape, BF16),
             pltpu.VMEM((shares - 1,) + coarse.shape, BF16),
             pltpu.VMEM((own_subs, rows), jnp.int32),
+            pltpu.VMEM(codebooks.shape, F32),
+            pltpu.VMEM((own_width, rows), BF16),
             pltpu.VMEM((shares * own_width, rows), BF16),
             pltpu.VMEM((8, rows), F32),
             pltpu.VMEM((HALVES, total // HALVES, LANES), F32),
@@ -470,8 +483,8 @@
             pltpu.VMEM((total // HALVES, width), F32),
             pltpu.VMEM((total // HALVES, LANES), F32),
             pltpu.VMEM((HALVES, shares, 8, total // HALVES), F32),
-            pltpu.VMEM((HALVES, shares, groups, short, LANES), BF16),
-            pltpu.VMEM((HALVES, shares - 1, groups, short, LANES), BF16),
+            pltpu.VMEM((HALVES, shares, groups, short, LANES), F32),
+            pltpu.VMEM((HALVES, shares - 1, groups, short, LANES), F32),
             pltpu.VMEM((HALVES, groups, short, LANES), F32),
             pltpu.VMEM((HALVES, groups, short, LANES), F32),
             pltpu.VMEM((groups, 8, LANES), F32),

time: 66.4 us -> 68.4 us (1.030)
  Pallas kernels: 63.1 us -> 65.2 us
    pallas_call x1, Pallas kernels: 63.1 us -> 65.2 us  [local(): pl.pallas_call(functools.partial(whole_kernel, groups, shares, half, row_...]
where the time goes in v4:
time: 68.4 us; the launch traced here: 68.2 us
  Pallas kernels  65.2 us (95%)
  local copies, waits for them, and re-layouts  1.66 us (2%)
  other arithmetic  1.38 us (2%)
    pallas_call x1, Pallas kernels, local(): pl.pallas_call(functools.partial(whole_kernel, groups, shares, half, row_...  65.2 us
    transpose x1, local copies, waits for them, and re-layouts, local(): return pooled.T  1.66 us
    transpose x1, other arithmetic, local(): jnp.concatenate([probe_groups, probe_cells.reshape(count, -1)], axis=1)  1.38 us

profile of v4, /device:TPU:0, one launch (start us, length us, event | category | flops | bytes accessed | tf_op | source)
XLA Modules:
  0.0 68.2 jit_solution(4250867558966246732)
XLA Ops:
  0.0 1.4 %add_bitcast_fusion.meta_ref = s32[34,256]{1,0:T(8,128)} fusion(s32[256,32]{0,1:T(8,128)} %bitcast.7, s32[256,2]{0,1:T(2,128)} %param.9), kind=kLoop, calls=%fused_computation | loop fusion | flops 8704 | bytes 69632 | tf_op jit(solution)/shard_map/transpose | solution.py:458
  1.4 65.2 %shard_map.82 = bf16[256,256]{1,0:T(8,128)(2,1)} custom-call(s32[34,256]{1,0:T(8,128)} %add_bitcast_fusion.meta_ref, bf16[256,256]{1,0:T(8,128)(2,1)} %rows_ref.1, s32[32,16,384]{2,1,0:T(8,128)} %raw_codes_ref.1, bf16[16,16,256]{2,1,0:T(8,128)(2,1)} %books_ref.1, bf16[32,256]{1,0:T(8,128)(2,1)} %coarse_ref.1, s32[32]{0:T(128)} %lengths_ref.1, ...), custom_call_target="tpu_custom_call" | custom-call | tf_op jit(solution)/shard_map/pallas_call | solution.py:461
  66.6 1.7 %copy.9 = bf16[256,256]{1,0:T(8,128)(2,1)} copy(bf16[256,256]{0,1:T(8,128)(2,1)} %bitcast.6) | data formatting | bytes 262144 | tf_op jit(solution)/shard_map/transpose | solution.py:500

commit v5 on v4

--- a/solution.py
+++ b/solution.py
@@ -33,11 +33,14 @@
     return first, second, routed, earlier
 
 
-def pack_kernel(groups, half, meta_ref, rows_ref, buffer_ref, away_ref):
+def pack_kernel(groups, half, cells, meta_ref, rows_ref, buffer_ref, away_ref):
     count = meta_ref.shape[1]
     first, second, routed, earlier = positions(meta_ref, groups)
     spot = routed * (earlier + 1.0) - 1.0
-    cell_ids = iota((LANES, count), 0)
+    cell_ids = lax.rem(iota((LANES, count), 0), cells)
+    folds = LANES // cells
+    short = CAP // folds
+    lane_group = iota((short, LANES), 1) // cells
 
     def named(start):
         marks = jnp.zeros((LANES, count), F32)
@@ -56,36 +59,53 @@
         there = lax.dot_general(
             onehot, marks.astype(BF16), (((1,), (1,)), ((), ())), preferred_element_type=F32
         )
-        away_ref[g] = (1.0 - there).astype(BF16)
-
-
-def decode_share(subs, width, blocks, codes_ref, books_ref, base, ids, tables, centers, vectors, squares):
+        packed = jnp.zeros((short, LANES), F32)
+        for b in range(folds):
+            packed = jnp.where(lane_group == b, there[b * short : (b + 1) * short], packed)
+        away_ref[g] = (1.0 - packed).astype(BF16)
+
+
+def look_up(table, index):
+    along = lax.GatherDimensionNumbers(
+        offset_dims=(),
+        collapsed_slice_dims=(1,),
+        start_index_map=(1,),
+        operand_batching_dims=(0,),
+        start_indices_batching_dims=(0,),
+    )
+    return lax.gather(
+        table,
+        index[..., None],
+        along,
+        slice_sizes=(1, 1),
+        mode=lax.GatherScatterMode.PROMISE_IN_BOUNDS,
+    )
+
+
+def decode_share(between, subs, width, blocks, codes_ref, books_ref, base, ids, centers, vectors, squares):
     near = min(8, subs)
     ids[...] = codes_ref[...].astype(F32).astype(jnp.int32)
-    tables[...] = books_ref[...].astype(F32)
     for start in range(0, subs, near):
+        between()
 
         @pl.loop(0, blocks // 2)
         def _(pair):
             for u in range(2):
                 lanes = pl.ds(pl.multiple_of(pair * (2 * LANES) + u * LANES, LANES), LANES)
                 inner = slice(start * width, (start + near) * width)
-                around = centers[inner, lanes].astype(F32)
+                around = centers[inner, lanes]
                 found = []
                 for j in range(start, start + near):
-                    code = jnp.broadcast_to(ids[j : j + 1, lanes], (8, LANES))
+                    code = jnp.broadcast_to(ids[j : j + 1, lanes], (width, LANES)).astype(jnp.int16)
                     index = code & (LANES - 1)
-                    for d in range(0, width, 8):
-                        low = tables[j, d : d + 8, :LANES]
-                        high = tables[j, d : d + 8, LANES:]
-                        found.append(
-                            jnp.where(
-                                code < LANES,
-                                jnp.take_along_axis(low, index, axis=1, mode="promise_in_bounds"),
-                                jnp.take_along_axis(high, index, axis=1, mode="promise_in_bounds"),
-                            )
+                    found.append(
+                        jnp.where(
+                            code < LANES,
+                            look_up(books_ref[j, :, :LANES], index),
+                            look_up(books_ref[j, :, LANES:], index),
                         )
-                summed = (jnp.concatenate(found, axis=0) + around).astype(BF16)
+                    )
+                summed = jnp.concatenate(found, axis=0) + around
                 vectors[base + start * width : base + (start + near) * width, lanes] = summed
                 back = summed.astype(F32)
                 back = back * back
@@ -104,18 +124,20 @@
     books_ref,
     coarse_ref,
     lengths_ref,
+    payload_hbm,
+    pooled_ref,
     payload_ref,
-    pooled_ref,
+    payload_sem,
     codes_ref,
     buffer,
     away_out,
     queries,
+    away_in,
     away,
     codes_in,
     books_in,
     coarse_in,
     ids,
-    tables,
     spread,
     vectors,
     squares,
@@ -141,7 +163,7 @@
     book_width = books_ref.shape[1]
     cells, own_width = coarse_ref.shape
     total = groups * CAP
-    width = payload_ref.shape[1]
+    width = payload_hbm.shape[1]
     own_columns = width // shares
     short = CAP // fold // HALVES
     blocks = rows // LANES
@@ -166,6 +188,8 @@
         return copy
 
     barrier = pltpu.get_barrier_semaphore()
+    table_copy = pltpu.make_async_copy(payload_hbm, payload_ref, payload_sem)
+    table_copy.start()
     for off in range(1, groups):
         pl.semaphore_signal(
             barrier, inc=1, device_id=device(off, 0), device_id_type=pl.DeviceIdType.MESH
@@ -174,6 +198,20 @@
         pl.semaphore_signal(
             barrier, inc=1, device_id=device(0, off), device_id_type=pl.DeviceIdType.MESH
         )
+    pack_kernel(groups, half, cells, meta_ref, rows_ref, buffer, away_out)
+    pl.semaphore_wait(barrier, groups + shares - 2)
+
+    everything = []
+    routed = [None]
+    for off in range(1, groups):
+        target = lax.rem(me_cell + off, groups)
+        routed.append(
+            [
+                send(buffer.at[target], queries.at[0, me_cell], off, 0),
+                send(away_out.at[target], away_in.at[me_cell], off, 0),
+            ]
+        )
+        everything += routed[-1]
     several = LANES // math.gcd(row_local, LANES)
     for t in range(shares):
         for start in range(0, cells, several):
@@ -184,20 +222,6 @@
                 ],
                 axis=1,
             ).astype(F32).astype(BF16)
-    pack_kernel(groups, half, meta_ref, rows_ref, buffer, away_out)
-    pl.semaphore_wait(barrier, groups + shares - 2)
-
-    everything = []
-    routed = [None]
-    for off in range(1, groups):
-        target = lax.rem(me_cell + off, groups)
-        routed.append(
-            [
-                send(buffer.at[target], queries.at[0, me_cell], off, 0),
-                send(away_out.at[target], away.at[me_cell], off, 0),
-            ]
-        )
-        everything += routed[-1]
     core = lax.rem(me_cell, 2)
     beside = (me_cell + 1 - 2 * core, me_sub)
     split = subs // 2
@@ -216,7 +240,7 @@
         everything += lists[-1]
 
     queries[0, me_cell] = buffer[me_cell]
-    away[me_cell] = away_out[me_cell]
+    away_in[me_cell] = away_out[me_cell]
     spread_out = []
 
     def forward(off):
@@ -231,7 +255,14 @@
 
     forward(0)
     squares[...] = jnp.zeros_like(squares)
-    passed = 1
+    waiting = sorted(range(1, groups), key=lambda off: min(off, groups - off))
+    pauses = [0]
+
+    def between():
+        if pauses[0] and waiting:
+            forward(waiting.pop(0))
+        pauses[0] += 1
+
     for k in range(shares):
         if k == 1:
             for off in range(1, shares):
@@ -254,6 +285,7 @@
             ).astype(BF16)
 
         decode_share(
+            between,
             subs,
             book_width,
             blocks,
@@ -261,15 +293,12 @@
             books_in.at[k - 1] if k else books_ref,
             k * own_width,
             ids,
-            tables,
             spread,
             vectors,
             squares,
         )
-        until = min(groups, 1 + -(-(groups - 1) * (k + 1) // min(shares, 2)))
-        for off in range(passed, until):
-            forward(off)
-        passed = max(passed, until)
+    while waiting:
+        forward(waiting.pop(0))
     everything += spread_out
 
     offset = iota((cells, rows), 1) - iota((cells, rows), 0) * row_local
@@ -286,6 +315,12 @@
     squares[0:1, :] = jnp.where(live > 0.5, half_norm, -floor_score)
     for copy in spread_out:
         copy.wait_recv()
+    folds = LANES // cells
+    deep = CAP // folds
+    lane_group = iota((groups, deep, LANES), 2) // cells
+    packed = away_in[...].astype(F32)
+    for b in range(folds):
+        away[:, b * deep : (b + 1) * deep] = jnp.where(lane_group == b, packed, 0.0).astype(BF16)
     part_cap = CAP // HALVES
     part_total = total // HALVES
 
@@ -296,7 +331,8 @@
         @pl.loop(0, rows // step)
         def _(n):
             lanes = pl.ds(pl.multiple_of(n * step, step), step)
-            shift = iota((LANES, step), 1) + n * step - iota((LANES, step), 0) * row_local
+            cell_of = lax.rem(iota((LANES, step), 0), cells)
+            shift = iota((LANES, step), 1) + n * step - cell_of * row_local
             far = jnp.where((shift >= 0) & (shift < row_local), floor_score, 0.0).astype(BF16)
             raw = jnp.dot(
                 away[:, some].reshape(part_total, LANES), far, preferred_element_type=F32
@@ -380,6 +416,7 @@
         return sent, jnp.where(iota((8, part_total), 0) == 0, mass_all, peak)
 
     tops = [score(h) for h in range(HALVES)]
+    table_copy.wait()
     pooled = [pool(h, tops[h]) for h in range(HALVES)]
     given = [give_back(h, *pooled[h]) for h in range(HALVES)]
     returned = []
@@ -461,19 +498,21 @@
     pooled = pl.pallas_call(
         functools.partial(whole_kernel, groups, shares, half, row_local, fold),
         out_shape=jax.ShapeDtypeStruct((width, count), BF16),
-        in_specs=[spec] * 5 + [pl.BlockSpec(memory_space=pltpu.SMEM), spec],
+        in_specs=[spec] * 5 + [pl.BlockSpec(memory_space=pltpu.SMEM), pl.BlockSpec(memory_space=pl.ANY)],
         out_specs=spec,
         scratch_shapes=[
+            pltpu.VMEM((rows, width), BF16),
+            pltpu.SemaphoreType.DMA,
             pltpu.VMEM((shares, own_subs, rows), BF16),
             pltpu.VMEM((groups, CAP, own_width), BF16),
-            pltpu.VMEM((groups, CAP, LANES), BF16),
+            pltpu.VMEM((groups, CAP * cells // LANES, LANES), BF16),
             pltpu.VMEM((shares, groups, CAP, own_width), BF16),
+            pltpu.VMEM((groups, CAP * cells // LANES, LANES), BF16),
             pltpu.VMEM((groups, CAP, LANES), BF16),
             pltpu.VMEM((shares - 1, own_subs, rows), BF16),
             pltpu.VMEM((shares - 1,) + codebooks.shape, BF16),
             pltpu.VMEM((shares - 1,) + coarse.shape, BF16),
             pltpu.VMEM((own_subs, rows), jnp.int32),
-            pltpu.VMEM(codebooks.shape, F32),
             pltpu.VMEM((own_width, rows), BF16),
             pltpu.VMEM((shares * own_width, rows), BF16),
             pltpu.VMEM((8, rows), F32),

time: 68.4 us -> 65.1 us (0.952)
  Pallas kernels: 65.2 us -> 61.8 us
    pallas_call x1, Pallas kernels: 65.2 us -> 61.8 us  [local(): pl.pallas_call(functools.partial(whole_kernel, groups, shares, half, row_...]
where the time goes in v5:
time: 65.1 us; the launch traced here: 64.9 us
  Pallas kernels  61.8 us (95%)
  local copies, waits for them, and re-layouts  1.66 us (3%)
  other arithmetic  1.38 us (2%)
    pallas_call x1, Pallas kernels, local(): pl.pallas_call(functools.partial(whole_kernel, groups, shares, half, row_...  61.8 us
    transpose x1, local copies, waits for them, and re-layouts, local(): return pooled.T  1.66 us
    transpose x1, other arithmetic, local(): jnp.concatenate([probe_groups, probe_cells.reshape(count, -1)], axis=1)  1.38 us

profile of v5, /device:TPU:0, one launch (start us, length us, event | category | flops | bytes accessed | tf_op | source)
XLA Modules:
  0.0 64.9 jit_solution(4026457526508739606)
XLA Ops:
  0.0 1.4 %add_bitcast_fusion.meta_ref = s32[34,256]{1,0:T(8,128)} fusion(s32[256,32]{0,1:T(8,128)} %bitcast.7, s32[256,2]{0,1:T(2,128)} %param.9), kind=kLoop, calls=%fused_computation | loop fusion | flops 8704 | bytes 69632 | tf_op jit(solution)/shard_map/transpose | solution.py:495
  1.4 61.8 %shard_map.82 = bf16[256,256]{1,0:T(8,128)(2,1)} custom-call(s32[34,256]{1,0:T(8,128)} %add_bitcast_fusion.meta_ref, bf16[256,256]{1,0:T(8,128)(2,1)} %rows_ref.1, s32[32,16,384]{2,1,0:T(8,128)} %raw_codes_ref.1, bf16[16,16,256]{2,1,0:T(8,128)(2,1)} %books_ref.1, bf16[32,256]{1,0:T(8,128)(2,1)} %coarse_ref.1, s32[32]{0:T(128)} %lengths_ref.1, ...), custom_call_target="tpu_custom_call" | custom-call | tf_op jit(solution)/shard_map/pallas_call | solution.py:498
  63.2 1.7 %copy.9 = bf16[256,256]{1,0:T(8,128)(2,1)} copy(bf16[256,256]{0,1:T(8,128)(2,1)} %bitcast.6) | data formatting | bytes 262144 | tf_op jit(solution)/shard_map/transpose | solution.py:539

commit v6 on v5

--- a/solution.py
+++ b/solution.py
@@ -139,6 +139,7 @@
     coarse_in,
     ids,
     spread,
+    joined,
     vectors,
     squares,
     best,
@@ -255,6 +256,15 @@
 
     forward(0)
     squares[...] = jnp.zeros_like(squares)
+
+    @pl.loop(0, rows // step)
+    def _(n):
+        lanes = pl.ds(pl.multiple_of(n * step, step), step)
+        cell_of = lax.rem(iota((LANES, step), 0), cells)
+        shift = iota((LANES, step), 1) + n * step - cell_of * row_local
+        far = jnp.where((shift >= 0) & (shift < row_local), floor_score, 0.0).astype(BF16)
+        vectors[shares * own_width :, lanes] = far
+
     waiting = sorted(range(1, groups), key=lambda off: min(off, groups - off))
     pauses = [0]
 
@@ -327,22 +337,16 @@
     def score(h):
         some = slice(h * part_cap, (h + 1) * part_cap)
         best[h] = jnp.full(best.shape[1:], 3.0 * floor_score, F32)
+        joined[h] = jnp.concatenate(
+            [queries[k, :, some].reshape(part_total, own_width) for k in range(shares)]
+            + [away[:, some].reshape(part_total, LANES)],
+            axis=1,
+        )
 
         @pl.loop(0, rows // step)
         def _(n):
             lanes = pl.ds(pl.multiple_of(n * step, step), step)
-            cell_of = lax.rem(iota((LANES, step), 0), cells)
-            shift = iota((LANES, step), 1) + n * step - cell_of * row_local
-            far = jnp.where((shift >= 0) & (shift < row_local), floor_score, 0.0).astype(BF16)
-            raw = jnp.dot(
-                away[:, some].reshape(part_total, LANES), far, preferred_element_type=F32
-            )
-            for k in range(shares):
-                raw = raw + jnp.dot(
-                    queries[k, :, some].reshape(part_total, own_width),
-                    vectors[k * own_width : (k + 1) * own_width, lanes],
-                    preferred_element_type=F32,
-                )
+            raw = jnp.dot(joined[h], vectors[:, lanes], preferred_element_type=F32)
             scores = (raw - squares[0:1, lanes]) * score_scale
             values[h, :, lanes] = scores
             top = best[h]
@@ -514,7 +518,8 @@
             pltpu.VMEM((shares - 1,) + coarse.shape, BF16),
             pltpu.VMEM((own_subs, rows), jnp.int32),
             pltpu.VMEM((own_width, rows), BF16),
-            pltpu.VMEM((shares * own_width, rows), BF16),
+            pltpu.VMEM((HALVES, total // HALVES, shares * own_width + LANES), BF16),
+            pltpu.VMEM((shares * own_width + LANES, rows), BF16),
             pltpu.VMEM((8, rows), F32),
             pltpu.VMEM((HALVES, total // HALVES, LANES), F32),
             pltpu.VMEM((HALVES, total // HALVES, rows), F32),

time: 65.1 us -> 65.1 us (level)
  no operation moved by 1% of the time
where the time goes in v6:
time: 65.1 us; the launch traced here: 64.9 us
  Pallas kernels  61.8 us (95%)
  local copies, waits for them, and re-layouts  1.66 us (3%)
  other arithmetic  1.38 us (2%)
    pallas_call x1, Pallas kernels, local(): pl.pallas_call(functools.partial(whole_kernel, groups, shares, half, row_...  61.8 us
    transpose x1, local copies, waits for them, and re-layouts, local(): return pooled.T  1.66 us
    transpose x1, other arithmetic, local(): jnp.concatenate([probe_groups, probe_cells.reshape(count, -1)], axis=1)  1.38 us

profile of v6, /device:TPU:0, one launch (start us, length us, event | category | flops | bytes accessed | tf_op | source)
XLA Modules:
  0.0 64.9 jit_solution(16085121614750893652)
XLA Ops:
  0.0 1.4 %add_bitcast_fusion.meta_ref = s32[34,256]{1,0:T(8,128)} fusion(s32[256,32]{0,1:T(8,128)} %bitcast.7, s32[256,2]{0,1:T(2,128)} %param.9), kind=kLoop, calls=%fused_computation | loop fusion | flops 8704 | bytes 69632 | tf_op jit(solution)/shard_map/transpose | solution.py:499
  1.4 61.8 %shard_map.82 = bf16[256,256]{1,0:T(8,128)(2,1)} custom-call(s32[34,256]{1,0:T(8,128)} %add_bitcast_fusion.meta_ref, bf16[256,256]{1,0:T(8,128)(2,1)} %rows_ref.1, s32[32,16,384]{2,1,0:T(8,128)} %raw_codes_ref.1, bf16[16,16,256]{2,1,0:T(8,128)(2,1)} %books_ref.1, bf16[32,256]{1,0:T(8,128)(2,1)} %coarse_ref.1, s32[32]{0:T(128)} %lengths_ref.1, ...), custom_call_target="tpu_custom_call" | custom-call | tf_op jit(solution)/shard_map/pallas_call | solution.py:502
  63.2 1.7 %copy.9 = bf16[256,256]{1,0:T(8,128)(2,1)} copy(bf16[256,256]{0,1:T(8,128)(2,1)} %bitcast.6) | data formatting | bytes 262144 | tf_op jit(solution)/shard_map/transpose | solution.py:544
